TPU v7x, 32 devices: a whole 2x2x4 slice. The times are simulated.
32 devices in a mesh: groups: 2 (over y), ctx: 16 (over z, x, core).
Axes of the slice: x: 2, y: 2, z: 4, core: 2. Of those that a mesh axis runs over, the one named last changes fastest.
Arguments:
- inputs: bfloat16 [8192, 7168], P(('groups', 'ctx')), parts along dimension 0, may hold values from -6 to 6
- out_grads: bfloat16 [8192, 7168], P(('groups', 'ctx')), parts along dimension 0, may hold values from -6 to 6
- gates: float32 [8192, 8], P(('groups', 'ctx')), parts along dimension 0, may hold values from 0.05 to 0.8
- expert_ids: int32 [8192, 8], P(('groups', 'ctx')), parts along dimension 0, may hold values from 0 to 255, all different within a row; in each aligned block of 256 rows (0 to 255, 256 to 511, ...) at most 24 rows name the same one
- offsets: int32 [18], P('groups'), parts along dimension 0, may hold values from 0 to 4096, as said below
- projections: bfloat16 [7168, 128], replicated, may hold values from -0.0625 to 0.0625
Outputs:
- shared_sketch: float32 [16, 4096], P('groups', 'ctx'), parts along dimension 0
- routed_sketch: float32 [256, 16, 4096], P('ctx', 'groups'), parts along dimension 1
There are 2 independent parts, one for each index of `groups`. A program takes and returns all parts, laid end to end along the dimension named above; an argument that names none is the same for every part. Nothing has to cross between parts.
Inputs may be any that keep to these rules, and one draw needn't show every extreme that they name: `expert_ids`: each row names 8 different experts. Within the 256 rows of one index of ctx no expert is named more than 24 times, and in every draw some expert is named exactly 24 times by the rows of some index. offsets[0] = 0, offsets[8] = 4096, strictly rising; every document holds more than 256 tokens.
All inputs are finite; a program needn't handle non-finite values.
Results may differ from a plain program's by a relative error of at most 0.0041.
Values may be sent and summed in bfloat16 or wider, within the bound.
No kernel may reach another device: no remote copies, remote signals or barrier semaphores. Data moves between devices by JAX's collectives and lax.ppermute only.
A program may use at most 128 MiB of HBM per device.

v0:
```python
import jax
import jax.numpy as jnp
from jax import lax
from jax.sharding import PartitionSpec as P

EXPERTS = 256
TOPK = 8
DOCS = 8
CAP = 24


def on_device(inputs, out_grads, gates, expert_ids, offsets, projections):
    tok_rows = inputs.shape[0]
    rank = projections.shape[1] // 2
    devices = lax.axis_size("ctx")
    local_experts = EXPERTS // devices
    a_rows = jnp.dot(inputs, projections[:, :rank], preferred_element_type=jnp.float32).astype(
        jnp.bfloat16
    )
    b_full = jnp.dot(out_grads, projections[:, rank:], preferred_element_type=jnp.float32)
    position = lax.axis_index("ctx") * tok_rows + jnp.arange(tok_rows, dtype=jnp.int32)
    doc = jnp.sum((position[:, None] >= offsets[None, 1:DOCS]).astype(jnp.int32), axis=1)
    lengths = (offsets[1:] - offsets[:-1]).astype(jnp.float32)
    doc_range = jnp.arange(DOCS, dtype=jnp.int32)
    doc_hot = doc[:, None] == doc_range[None, :]
    length_tok = jnp.sum(jnp.where(doc_hot, lengths[None, :], jnp.zeros((), jnp.float32)), axis=1)
    inverse = lax.rsqrt(length_tok)
    shared_rows = (b_full * inverse[:, None]).astype(jnp.bfloat16)
    route_scale = (EXPERTS / TOPK) ** 0.5
    routed = (
        gates[:, :, None] * (route_scale * inverse)[:, None, None] * b_full[:, None, :]
    ).astype(jnp.bfloat16)
    masked = jnp.where(
        doc_hot[:, :, None], shared_rows[:, None, :], jnp.zeros((), jnp.bfloat16)
    ).reshape(tok_rows, DOCS * rank)
    shared_part = lax.dot_general(
        masked, a_rows, (((0,), (0,)), ((), ())), preferred_element_type=jnp.float32
    )
    shared_sketch = lax.psum_scatter(
        shared_part.reshape(DOCS, rank * rank), "ctx", scatter_dimension=1, tiled=True
    )
    flat_ids = expert_ids.reshape(-1)
    expert_hot = (flat_ids[:, None] == jnp.arange(EXPERTS, dtype=jnp.int32)[None, :]).astype(
        jnp.int32
    )
    earlier = jnp.cumsum(expert_hot, axis=0) - expert_hot
    slot = jnp.sum(earlier * expert_hot, axis=1)
    target = flat_ids * CAP + slot
    payload = jnp.concatenate(
        [routed.reshape(tok_rows * TOPK, rank), jnp.repeat(a_rows, TOPK, axis=0)], axis=1
    )
    buffer = (
        jnp.zeros((EXPERTS * CAP, 2 * rank), jnp.bfloat16)
        .at[target]
        .set(payload)
        .reshape(EXPERTS, CAP, 2 * rank)
    )
    doc_buffer = (
        jnp.zeros((EXPERTS * CAP,), jnp.int32)
        .at[target]
        .set(jnp.repeat(doc, TOPK))
        .reshape(EXPERTS, CAP)
    )
    got_rows, got_docs = (
        lax.all_to_all(buffer, "ctx", split_axis=0, concat_axis=0, tiled=True),
        lax.all_to_all(doc_buffer, "ctx", split_axis=0, concat_axis=0, tiled=True),
    )
    got_rows = got_rows.reshape(devices, local_experts, CAP, 2 * rank).transpose(1, 0, 2, 3)
    got_rows = got_rows.reshape(local_experts, devices * CAP, 2 * rank)
    got_docs = (
        got_docs.reshape(devices, local_experts, CAP)
        .transpose(1, 0, 2)
        .reshape(local_experts, devices * CAP)
    )
    owner_hot = got_docs[:, :, None] == doc_range[None, None, :]
    spread = jnp.where(
        owner_hot[:, :, :, None], got_rows[:, :, None, :rank], jnp.zeros((), jnp.bfloat16)
    )
    spread = spread.reshape(local_experts, devices * CAP, DOCS * rank)
    summed = jnp.einsum(
        "erm,erq->emq", spread, got_rows[:, :, rank:], preferred_element_type=jnp.float32
    )
    routed_sketch = summed.reshape(local_experts, DOCS, rank * rank)
    return (shared_sketch, routed_sketch)


def solution(mesh):
    placed = (
        P(("groups", "ctx"), None),
        P(("groups", "ctx"), None),
        P(("groups", "ctx"), None),
        P(("groups", "ctx"), None),
        P("groups"),
        P(),
    )
    return jax.shard_map(
        on_device,
        mesh=mesh,
        in_specs=placed,
        out_specs=(P("groups", "ctx"), P("ctx", "groups", None)),
        check_vma=False,
    )
```

profile of v0, /device:TPU:0, one launch (start us, length us, event | category | flops | bytes accessed | tf_op | source)
XLA Modules:
  0.0 120.4 jit_solution(15941819979806062061)
XLA Ops:
  7.2 0.7 broadcast_multiply_fusion.1
  7.9 0.8 copy.46
  8.7 0.1 eq.68
  8.8 0.1 eq.64
  8.9 0.7 slice.27
  9.6 0.1 copy.45
  9.8 0.1 mul.72
  9.9 0.1 convert_reduce_fusion
  10.0 0.1 eq.61
  10.1 0.1 reshape.148
  10.2 0.1 copy.48
  10.3 0.3 fusion.2
  10.7 0.2 broadcast_add_fusion
  10.9 1.2 %copy.49 = s32[256,16,128]{0,2,1:T(8,128)S(1)} copy(s32[256,16,128]{0,1,2:T(8,128)S(1)} %broadcast_add_fusion) | data formatting | bytes 4194304 | tf_op jit(solution)/shard_map/reduce_window_sum
  12.2 0.0 copy-start.2
  12.2 0.0 copy-start
  12.2 0.9 fusion.1
  13.2 8.1 %scatter_custom_fusion = s32[6144]{0:T(1024)S(1)} fusion(s32[2048]{0:T(1024)S(1)} %bitcast.41, s32[2048]{0:T(1024)S(1)} %reshape.148, s32[]{:T(128)} %constant.10.clone.1), kind=kCustom, calls=%fused_computation.34 | custom fusion | bytes 24580 | tf_op jit(solution)/shard_map/scatter | solution.py:61
  21.3 0.1 all_to_all.9
  21.4 0.7 reshape.164
  22.1 7.4 %all-to-all-start = ((s32[16,1,384]{2,1,0:T(1,128)}), s32[16,1,384]{2,1,0:T(1,128)S(1)}, u32[]{:S(2)}, u32[]{:S(2)}) async-start(s32[16,1,384]{2,1,0:T(1,128)} %reshape.164), calls=%async_computation.1 | async-start | bytes 49152 | tf_op jit(solution)/shard_map/all_to_all | solution.py:66
  29.5 0.0 copy-done.2
  29.5 0.1 subtract_convert_fusion
  29.5 0.2 select_reduce_fusion
  29.7 0.0 copy-done
  29.7 0.0 copy-start.1
  29.8 3.3 %fusion.10 = bf16[256,64]{0,1:T(8,128)(2,1)S(1)} fusion(bf16[256,7168]{1,0:T(8,128)(2,1)} %param.6, bf16[7168,128]{1,0:T(8,128)(2,1)S(1)} %copy-done), kind=kOutput, calls=%fused_computation.16 | convolution fusion | flops 234897408 | bytes 5537792 | tf_op jit(solution)/shard_map/dot_general | solution.py:17
  33.0 0.1 copy.53
  33.2 0.0 copy-done.1
  33.2 0.1 copy.51
  33.3 0.1 mul.78
  33.4 4.2 %multiply_convert_fusion = (bf16[256,64]{0,1:T(8,128)(2,1)S(1)}, f32[256,64]{0,1:T(8,128)S(1)}) fusion(f32[256]{0:T(256)S(1)} %get-tuple-element.3, bf16[256,7168]{1,0:T(8,128)(2,1)} %param.7, bf16[7168,128]{1,0:T(8,128)(2,1)S(1)} %copy-done), kind=kOutput, calls=%fused_computation.31 | convolution fusion | flops 234913792 | bytes 5604352 | tf_op jit(solution)/shard_map/dot_general | solution.py:20
  37.6 0.1 copy.52
  37.7 0.3 fusion.13
  38.1 0.1 broadcast_bitcast_fusion
  38.1 7.5 %scatter_custom_fusion.1 = bf16[6144,128]{1,0:T(8,128)(2,1)} fusion(s32[2048]{0:T(1024)S(1)} %bitcast.42, bf16[]{:T(256)} %constant.12.clone.1, bf16[2048,64]{1,0:T(8,128)(2,1)S(1)} %broadcast_bitcast_fusion, bf16[]{:T(256)} %constant.26, bf16[2048,64]{1,0:T(8,128)(2,1)S(1)} %fusion.13), kind=kCustom, calls=%fused_computation.21 | custom fusion | flops 1048576 | bytes 2621444 | tf_op jit(solution)/shard_map/scatter | solution.py:55
  45.7 0.0 all-to-all-done
  45.7 6.0 %all-to-all-start.1 = ((bf16[256,24,128]{2,1,0:T(8,128)(2,1)}), bf16[256,24,128]{2,1,0:T(8,128)(2,1)S(1)}, u32[]{:S(2)}, u32[]{:S(2)}) async-start(bf16[256,24,128]{2,1,0:T(8,128)(2,1)} %bitcast.9), calls=%async_computation.2 | async-start | bytes 3145728 | tf_op jit(solution)/shard_map/all_to_all | solution.py:65
  51.7 0.2 reduce-scatter.2.cloned.1.call-start
  51.9 0.1 iota_compare_fusion.4
  52.0 0.1 copy.43
  52.2 0.2 fusion.22
  52.4 0.8 reshape.136
  53.1 0.0 reduce-scatter.2.cloned.1.call-update
  53.1 0.6 broadcast.97
  53.7 0.7 reduce
  54.5 0.1 reshape.165
  54.7 0.1 eq.72
  54.8 28.9 %all-to-all-done.1 = bf16[256,24,128]{2,1,0:T(8,128)(2,1)S(1)} async-done(((bf16[256,24,128]{2,1,0:T(8,128)(2,1)}), bf16[256,24,128]{2,1,0:T(8,128)(2,1)S(1)}, u32[]{:S(2)}, u32[]{:S(2)}) %all-to-all-start.1) | async-done | bytes 1572896 | tf_op jit(solution)/shard_map/all_to_all | solution.py:65
  83.7 0.4 copy.54
  84.1 0.7 copy.55
  84.8 0.8 broadcast_select_fusion
  85.6 3.8 %fusion.8 = f32[16,512,64]{2,1,0:T(8,128)} fusion(bf16[16,384,512]{1,2,0:T(8,128)(2,1)S(1)} %bitcast.34, bf16[16,384,128]{2,1,0:T(8,128)(2,1)S(1)} %bitcast.36), kind=kOutput, calls=%fused_computation.14 | convolution fusion | flops 402653184 | bytes 9961472 | tf_op jit(solution)/shard_map/erm,erq->emq/dot_general | solution.py:80
  89.4 4.8 %reshape.143 = f32[16,8,4096]{2,1,0:T(8,128)} reshape(f32[16,512,64]{2,1,0:T(8,128)} %fusion.8) | data formatting | bytes 4194304 | tf_op jit(solution)/shard_map/reshape | solution.py:83
  94.2 19.3 %reduce-scatter.2.cloned.1.call-done = f32[8,256]{1,0:T(8,128)} async-done(((f32[8,4096]{1,0:T(8,128)}), f32[8,256]{1,0:T(8,128)}) %reduce-scatter.2.cloned.1.call-update) | async-done | bytes 8208 | tf_op jit(solution)/shard_map/reduce_scatter | solution.py:39
  (10 shorter events, 0.2 us)
Async XLA Ops:
  12.2 17.3 %copy-start.2 = (s32[9]{0:T(128)S(1)}, s32[9]{0:T(128)}, u32[]{:S(2)}) copy-start(s32[9]{0:T(128)} %param.10) | copy-start | bytes 112
  12.2 17.6 %copy-start = (bf16[7168,128]{1,0:T(8,128)(2,1)S(1)}, bf16[7168,128]{1,0:T(8,128)(2,1)}, u32[]{:S(2)}) copy-start(bf16[7168,128]{1,0:T(8,128)(2,1)} %param.11) | copy-start | bytes 5505028
  22.1 23.6 %all-to-all-start = ((s32[16,1,384]{2,1,0:T(1,128)}), s32[16,1,384]{2,1,0:T(1,128)S(1)}, u32[]{:S(2)}, u32[]{:S(2)}) async-start(s32[16,1,384]{2,1,0:T(1,128)} %reshape.164), calls=%async_computation.1 | async-start | bytes 49152 | tf_op jit(solution)/shard_map/all_to_all | solution.py:66
  29.7 3.4 %copy-start.1 = (f32[256,8]{0,1:T(8,128)S(1)}, f32[256,8]{0,1:T(8,128)}, u32[]{:S(2)}) copy-start(f32[256,8]{0,1:T(8,128)} %param.8) | copy-start | bytes 24580
  45.7 38.0 %all-to-all-start.1 = ((bf16[256,24,128]{2,1,0:T(8,128)(2,1)}), bf16[256,24,128]{2,1,0:T(8,128)(2,1)S(1)}, u32[]{:S(2)}, u32[]{:S(2)}) async-start(bf16[256,24,128]{2,1,0:T(8,128)(2,1)} %bitcast.9), calls=%async_computation.2 | async-start | bytes 3145728 | tf_op jit(solution)/shard_map/all_to_all | solution.py:65
  51.7 61.8 %reduce-scatter.2.cloned.1.call-start = ((), (), s32[]{:S(2)}) async-start(), calls=%async_computation.3 | async-start | bytes 139264 | tf_op jit(solution)/shard_map/reduce_scatter | solution.py:39
Sparse Core Ops, SparseCore 0:
  56.6 56.9 reduce-scatter.1
where the time goes:
time: 121 us; the launch traced here: 120 us
  waiting for transfers between devices  48.2 us (40%)
  local copies, waits for them, and re-layouts  20.6 us (17%)
  between operations  14.3 us (12%)
  starting transfers between devices  13.6 us (11%)
  other arithmetic  12.2 us (10%)
  matrix products  11.5 us (10%)
    all_to_all x1, waiting for transfers between devices, on_device(): lax.all_to_all(buffer, 'ctx', split_axis=0, concat_axis=0, tiled=True)  28.9 us
    reduce_scatter x1, waiting for transfers between devices, on_device(): lax.psum_scatter(shared_part.reshape(DOCS, rank * rank), 'ctx', scatter_d...  19.3 us
    scatter x1, local copies, waits for them, and re-layouts, on_device(): doc_buffer = jnp.zeros((EXPERTS * CAP,), jnp.int32).at[target].set(jnp.re...  8.08 us
    scatter x1, other arithmetic, on_device(): buffer = jnp.zeros((EXPERTS * CAP, 2 * rank), jnp.bfloat16).at[target].se...  7.54 us
    all_to_all x1, starting transfers between devices, on_device(): lax.all_to_all(doc_buffer, 'ctx', split_axis=0, concat_axis=0, tiled=True)  7.36 us
    all_to_all x1, starting transfers between devices, on_device(): lax.all_to_all(buffer, 'ctx', split_axis=0, concat_axis=0, tiled=True)  6 us
    reshape x1, local copies, waits for them, and re-layouts, on_device(): routed_sketch = summed.reshape(local_experts, DOCS, rank * rank)  4.8 us
    dot_general x1, matrix products, on_device(): jnp.dot(out_grads, projections[:, rank:], preferred_element_type=jnp.floa...  4.19 us
  transfers between devices with their start and end apart: 3, of which 2 were waited for; matrix products, arithmetic and copies ran while one was open for 24% of the time, Pallas kernels for 0%

commit v1 on v0

v1 whole, which is shorter than its diff:
```python
import functools

import jax
import jax.numpy as jnp
from jax import lax
from jax.experimental import pallas as pl
from jax.experimental.pallas import tpu as pltpu
from jax.sharding import PartitionSpec as P

EXPERTS = 256
TOPK = 8
DOCS = 8
CHUNK = 1024
VMEM_LIMIT = 48 * 1024 * 1024


def doc_of(offsets_ref, start):
    doc = jnp.int32(0)
    for i in range(1, DOCS):
        doc = doc + (start >= offsets_ref[i]).astype(jnp.int32)
    return doc


def project_kernel(
    where_ref, offsets_ref, gates_ref, ids_ref, x_hbm, g_hbm, p_hbm, out_ref,
    x_buf, g_buf, p_buf, rows_buf, x_sem, g_sem, p_sem,
):
    tok, depth = x_hbm.shape
    rank = p_hbm.shape[1] // 2
    half = rank // 2
    chunks = depth // CHUNK

    def copies(i):
        cols = pl.ds(i * CHUNK, CHUNK)
        return (
            pltpu.make_async_copy(p_hbm.at[cols, :], p_buf.at[cols, :], p_sem.at[i]),
            pltpu.make_async_copy(x_hbm.at[:, cols], x_buf.at[:, cols], x_sem.at[i]),
            pltpu.make_async_copy(g_hbm.at[:, cols], g_buf.at[:, cols], g_sem.at[i]),
        )

    for i in range(chunks):
        for copy in copies(i):
            copy.start()
    a = jnp.zeros((tok, rank), jnp.float32)
    b = jnp.zeros((tok, rank), jnp.float32)
    for i in range(chunks):
        for copy in copies(i):
            copy.wait()
        cols = pl.ds(i * CHUNK, CHUNK)
        a = a + jnp.dot(
            x_buf[:, cols], p_buf[cols, :rank], preferred_element_type=jnp.float32
        )
        b = b + jnp.dot(
            g_buf[:, cols], p_buf[cols, rank:], preferred_element_type=jnp.float32
        )
    start = where_ref[0]
    first = doc_of(offsets_ref, start)
    second = jnp.minimum(first + 1, DOCS - 1)
    position = start + lax.broadcasted_iota(jnp.int32, (1, tok), 1)
    in_first = position < offsets_ref[first + 1]
    length = jnp.where(
        in_first,
        offsets_ref[first + 1] - offsets_ref[first],
        offsets_ref[second + 1] - offsets_ref[second],
    ).astype(jnp.float32)
    scale = lax.rsqrt(length)
    both = jnp.concatenate([a, b], axis=1).T
    out_ref[:rank, :] = both[:rank, :].astype(jnp.bfloat16)
    scaled = both[rank:, :] * scale
    for j in range(tok // 128):
        lanes = slice(j * 128, (j + 1) * 128)
        rows_buf[j, :, :] = scaled[:, lanes]
        for odd in range(2):
            picked = rows_buf[j, pl.ds(odd, half, stride=2), :]
            place = rank + odd * half
            out_ref[place : place + half, lanes] = picked.astype(jnp.bfloat16)
    gates = gates_ref[...]
    high = gates.astype(jnp.bfloat16).astype(jnp.float32)
    ids = ids_ref[...].astype(jnp.float32)
    out_ref[2 * rank : 2 * rank + 16, :] = jnp.concatenate([ids, high], axis=0).astype(jnp.bfloat16)
    out_ref[2 * rank + 16 :, :] = jnp.concatenate(
        [gates - high, jnp.zeros_like(gates)], axis=0
    ).astype(jnp.bfloat16)


def sum_kernel(
    experts, where_ref, offsets_ref, own_ref, other_ref, routed_ref, shared_ref, acc, tiles
):
    height, tok = 160, own_ref.shape[1]
    slots = own_ref.shape[0] // height
    rank = 64
    half = rank // 2
    me = where_ref[0]
    route_scale = (EXPERTS / TOPK) ** 0.5
    acc[...] = jnp.zeros_like(acc)

    def block(ref, source, base):
        start = source * tok
        first = doc_of(offsets_ref, start)
        edge = offsets_ref[first + 1]
        position = start + lax.broadcasted_iota(jnp.int32, (1, tok), 1)
        in_first = (position < edge).astype(jnp.float32)
        a = ref[pl.ds(base, rank), :].astype(jnp.float32)
        b = ref[pl.ds(base + rank, rank), :].astype(jnp.float32)
        named = ref[pl.ds(base + 2 * rank, 16), :].astype(jnp.float32)
        low = ref[pl.ds(base + 2 * rank + 16, 16), :].astype(jnp.float32)
        ids, gates = named[:8, :], (named[8:, :] + low[:8, :]) * route_scale
        even, odd = b[:half, :], b[half:, :]
        left = []
        for e in range(experts):
            mine = (me * experts + e).astype(jnp.float32)
            w = jnp.sum(jnp.where(ids == mine, gates, 0.0), axis=0, keepdims=True)
            left.append(jnp.concatenate([w * even, w * odd], axis=1).astype(jnp.bfloat16))
        left.append(jnp.concatenate([even, odd], axis=1).astype(jnp.bfloat16))
        left = jnp.concatenate(left, axis=0)
        a_first = a * in_first
        a_second = a - a_first
        none = jnp.zeros_like(a)
        right = jnp.concatenate(
            [
                jnp.concatenate([a_first, none], axis=1),
                jnp.concatenate([none, a_first], axis=1),
                jnp.concatenate([a_second, none], axis=1),
                jnp.concatenate([none, a_second], axis=1),
            ],
            axis=0,
        ).astype(jnp.bfloat16)
        both = lax.dot_general(
            left, right, (((1,), (1,)), ((), ())), preferred_element_type=jnp.float32
        )
        acc[first, :, :] += both[:, : 2 * rank]

        @pl.when(edge < start + tok)
        def _():
            acc[first + 1, :, :] += both[:, 2 * rank :]

    def step(s, _):
        base = pl.multiple_of(s * height, height)
        block(own_ref, where_ref[1 + s], base)
        block(other_ref, where_ref[1 + slots + s], base)
        return 0

    lax.fori_loop(0, slots, step, 0)
    rows = acc.shape[1]
    for d in range(DOCS):
        tiles[pl.ds(d, rows, stride=DOCS), :] = acc[d, :, :]
    for e in range(experts):
        for r in range(half):
            row = (e * half + r) * DOCS
            routed_ref[e, :, r * 128 : (r + 1) * 128] = tiles[row : row + DOCS, :]
    wide = shared_ref.shape[1] // 128
    place = experts * half + where_ref[1 + 2 * slots]
    for j in range(wide):
        row = pl.multiple_of((place + j) * DOCS, DOCS)
        shared_ref[:, j * 128 : (j + 1) * 128] = tiles[pl.ds(row, DOCS), :]


def on_device(devices, inputs, out_grads, gates, expert_ids, offsets, projections):
    tok, _ = inputs.shape
    rank = projections.shape[1] // 2
    half = rank // 2
    experts = EXPERTS // devices
    me = lax.axis_index("ctx").astype(jnp.int32)
    height = 2 * rank + 32
    smem = pl.BlockSpec(memory_space=pltpu.SMEM)
    vmem = pl.BlockSpec(memory_space=pltpu.VMEM)
    hbm = pl.BlockSpec(memory_space=pl.ANY)
    chunks = inputs.shape[1] // CHUNK
    payload = pl.pallas_call(
        project_kernel,
        out_shape=jax.ShapeDtypeStruct((height, tok), jnp.bfloat16),
        in_specs=[smem, smem, vmem, vmem, hbm, hbm, hbm],
        out_specs=vmem,
        scratch_shapes=[
            pltpu.VMEM(inputs.shape, jnp.bfloat16),
            pltpu.VMEM(inputs.shape, jnp.bfloat16),
            pltpu.VMEM(projections.shape, jnp.bfloat16),
            pltpu.VMEM((tok // 128, rank, 128), jnp.float32),
            pltpu.SemaphoreType.DMA((chunks,)),
            pltpu.SemaphoreType.DMA((chunks,)),
            pltpu.SemaphoreType.DMA((chunks,)),
        ],
        compiler_params=pltpu.CompilerParams(vmem_limit_bytes=VMEM_LIMIT),
        name="project",
    )((me * tok).reshape(1), offsets, gates.T, expert_ids.T, inputs, out_grads, projections)

    far = [1 << k for k in range(devices.bit_length() - 2, 0, -1)]
    order = (far, far[:1] + far[-1:] + far[1:-1] if len(far) > 2 else far)
    held, mask = payload, jnp.zeros((1,), jnp.int32)
    odd = (me & 1) == 1
    for k in range(len(far)):
        pairs = [(i, i ^ order[i & 1][k]) for i in range(devices)]
        got = lax.ppermute(held, "ctx", pairs)
        held = jnp.concatenate([held, got], axis=0)
        step = jnp.where(odd, order[1][k], order[0][k]).astype(jnp.int32)
        mask = jnp.concatenate([mask, mask ^ step])
    other = lax.ppermute(held, "ctx", [(i, i ^ 1) for i in range(devices)])
    other_mask = jnp.zeros((1,), jnp.int32)
    for k in range(len(far)):
        step = jnp.where(odd, order[0][k], order[1][k]).astype(jnp.int32)
        other_mask = jnp.concatenate([other_mask, other_mask ^ step])
    columns = rank * rank // devices
    where = jnp.concatenate(
        [me.reshape(1), me ^ mask, me ^ other_mask ^ 1, (me * columns // 128).reshape(1)]
    )
    rows = (experts + 1) * half
    routed, shared = pl.pallas_call(
        functools.partial(sum_kernel, experts),
        out_shape=(
            jax.ShapeDtypeStruct((experts, DOCS, rank * rank), jnp.float32),
            jax.ShapeDtypeStruct((DOCS, max(columns, 128)), jnp.float32),
        ),
        in_specs=[smem, smem, vmem, vmem],
        out_specs=(vmem, vmem),
        scratch_shapes=[
            pltpu.VMEM((DOCS, rows, 2 * rank), jnp.float32),
            pltpu.VMEM((DOCS * rows, 2 * rank), jnp.float32),
        ],
        compiler_params=pltpu.CompilerParams(vmem_limit_bytes=VMEM_LIMIT),
        name="sums",
    )(where, offsets, held, other)
    if columns < 128:
        shared = lax.dynamic_slice_in_dim(shared, me * columns % 128, columns, 1)
    return shared, routed


def solution(mesh):
    placed = (
        P(("groups", "ctx"), None),
        P(("groups", "ctx"), None),
        P(("groups", "ctx"), None),
        P(("groups", "ctx"), None),
        P("groups"),
        P(),
    )
    return jax.shard_map(
        functools.partial(on_device, mesh.shape["ctx"]),
        mesh=mesh,
        in_specs=placed,
        out_specs=(P("groups", "ctx"), P("ctx", "groups", None)),
        check_vma=False,
    )
```

time: 121 us -> 45.1 us (0.37)
  waiting for transfers between devices: 48.2 us -> 15.9 us
  Pallas kernels: 0 us -> 15.5 us
  local copies, waits for them, and re-layouts: 20.6 us -> 5.58 us
  between operations: 14.3 us -> 0.7 us
  other arithmetic: 12.2 us -> 0.4 us
  matrix products: 11.5 us -> 0 us
  starting transfers between devices: 13.6 us -> 6.7 us
    all_to_all x2 -> x0, waiting for transfers between devices: 28.9 us -> none  [the longest x1 28.9 us: on_device(): lax.all_to_all(buffer, 'ctx', split_axis=0, concat_axis=0, tiled=True)]
    reduce_scatter x1 -> x0, waiting for transfers between devices: 19.3 us -> none  [on_device(): lax.psum_scatter(shared_part.reshape(DOCS, rank * rank), 'ctx', scatter_d...]
    ppermute x0 -> x4, waiting for transfers between devices: none -> 15.9 us  [the longest x3 14.2 us: on_device(): got = lax.ppermute(held, 'ctx', pairs)]
    pallas_call x0 -> x2, Pallas kernels: none -> 15.5 us  [the longest x1 10.5 us: on_device(): pl.pallas_call(functools.partial(sum_kernel, experts), out_shape=(jax.Sha...]
    all_to_all x2 -> x0, starting transfers between devices: 13.4 us -> none  [the longest x1 7.36 us: on_device(): lax.all_to_all(doc_buffer, 'ctx', split_axis=0, concat_axis=0, tiled=True)]
    dot_general x4 -> x0, matrix products: 11.5 us -> none  [the longest x1 4.19 us: on_device(): jnp.dot(out_grads, projections[:, rank:], preferred_element_type=jnp.floa...]
    scatter x1 -> x0, local copies, waits for them, and re-layouts: 8.08 us -> none  [on_device(): doc_buffer = jnp.zeros((EXPERTS * CAP,), jnp.int32).at[target].set(jnp.re...]
    scatter x1 -> x0, other arithmetic: 7.54 us -> none  [on_device(): buffer = jnp.zeros((EXPERTS * CAP, 2 * rank), jnp.bfloat16).at[target].se...]
  transfers between devices with their start and end apart: 3 -> 4, of which waited for: 2 -> 4; matrix products, arithmetic and copies ran while one was open for 24% -> 1% of each run, Pallas kernels for 0% -> 0%
where the time goes in v1:
time: 45.1 us; the launch traced here: 44.8 us
  waiting for transfers between devices  15.9 us (35%)
  Pallas kernels  15.5 us (34%)
  starting transfers between devices  6.7 us (15%)
  local copies, waits for them, and re-layouts  5.58 us (12%)
  between operations  0.7 us (2%)
    ppermute x3, waiting for transfers between devices, on_device(): got = lax.ppermute(held, 'ctx', pairs)  14.2 us
    pallas_call x1, Pallas kernels, on_device(): pl.pallas_call(functools.partial(sum_kernel, experts), out_shape=(jax.Sha...  10.5 us
    ppermute x3, starting transfers between devices, on_device(): got = lax.ppermute(held, 'ctx', pairs)  6.63 us
    unnamed x12, local copies, waits for them, and re-layouts  5.58 us
    pallas_call x1, Pallas kernels, on_device(): pl.pallas_call(project_kernel, out_shape=jax.ShapeDtypeStruct((height, to...  5.03 us
    ppermute x1, waiting for transfers between devices, on_device(): other = lax.ppermute(held, 'ctx', [(i, i ^ 1) for i in range(devices)])  1.75 us
  transfers between devices with their start and end apart: 4, of which 4 were waited for; matrix products, arithmetic and copies ran while one was open for 1% of the time, Pallas kernels for 0%

profile of v1, /device:TPU:0, one launch (start us, length us, event | category | flops | bytes accessed | tf_op | source)
XLA Modules:
  0.0 44.8 jit_solution(4706011979608551721)
XLA Ops:
  0.6 0.0 copy-start
  0.6 2.0 %copy-done = bf16[256,7168]{1,0:T(8,128)(2,1)S(1)} copy-done((bf16[256,7168]{1,0:T(8,128)(2,1)S(1)}, bf16[256,7168]{1,0:T(8,128)(2,1)}, u32[]{:S(2)}) %copy-start) | copy-done | bytes 3670040
  2.7 0.0 copy-start.1
  2.7 1.5 %copy-done.1 = bf16[7168,128]{1,0:T(8,128)(2,1)S(1)} copy-done((bf16[7168,128]{1,0:T(8,128)(2,1)S(1)}, bf16[7168,128]{1,0:T(8,128)(2,1)}, u32[]{:S(2)}) %copy-start.1) | copy-done | bytes 1835032
  4.2 0.0 copy-start.2
  4.2 0.7 %copy-done.2 = f32[256,8]{0,1:T(8,128)S(1)} copy-done((f32[256,8]{0,1:T(8,128)S(1)}, f32[256,8]{0,1:T(8,128)}, u32[]{:S(2)}) %copy-start.2) | copy-done | bytes 8216
  4.9 0.0 copy-start.3
  4.9 0.7 %copy-done.3 = s32[256,8]{0,1:T(8,128)S(1)} copy-done((s32[256,8]{0,1:T(8,128)S(1)}, s32[256,8]{0,1:T(8,128)}, u32[]{:S(2)}) %copy-start.3) | copy-done | bytes 8216
  5.6 0.0 copy-start.4
  5.6 0.7 %copy-done.4 = s32[9]{0:T(128)S(1)} copy-done((s32[9]{0:T(128)S(1)}, s32[9]{0:T(128)}, u32[]{:S(2)}) %copy-start.4) | copy-done | bytes 60
  6.2 5.0 %project.1 = bf16[160,256]{1,0:T(8,128)(2,1)S(1)} custom-call(s32[1]{0:T(128)} %bitcast.2.where_ref, s32[9]{0:T(128)S(1)} %copy-done.4, f32[8,256]{1,0:T(8,128)S(1)} %bitcast.5, s32[8,256]{1,0:T(8,128)S(1)} %bitcast.6, bf16[256,7168]{1,0:T(8,128)(2,1)S(1)} %copy-done, bf16[256,7168]{1,0:T(8,128)(2,1)} %g_hbm.1, bf16[7168,128]{1,0:T(8,128)(2,1)S(1)} %copy-done.1), custom_call_target="tpu_custom_call" | custom-call | tf_op jit(solution)/shard_map/project/pallas_call | solution.py:169
  11.3 0.0 copy-start.5
  11.3 4.1 %collective-permute-start = (bf16[160,256]{1,0:T(8,128)(2,1)S(1)}, bf16[160,256]{1,0:T(8,128)(2,1)S(1)}, u32[]{:S(2)}, u32[]{:S(2)}) collective-permute-start(bf16[160,256]{1,0:T(8,128)(2,1)S(1)} %project.1), channel_id=1, source_target_pairs={{0,8},{1,9},{2,10},{3,11},{4,12},{5,13},{6,14},{7,15},{8,0},{9,1},... | collective-permute-start | bytes 245768 | tf_op jit(solution)/shard_map/ppermute | solution.py:193
  15.4 4.2 %collective-permute-done = bf16[160,256]{1,0:T(8,128)(2,1)S(1)} collective-permute-done((bf16[160,256]{1,0:T(8,128)(2,1)S(1)}, bf16[160,256]{1,0:T(8,128)(2,1)S(1)}, u32[]{:S(2)}, u32[]{:S(2)}) %collective-permute-start) | collective-permute-done | bytes 81952 | tf_op jit(solution)/shard_map/ppermute | solution.py:193
  19.6 0.8 %collective-permute-start.1 = (bf16[320,256]{1,0:T(8,128)(2,1)S(1)}, bf16[320,256]{1,0:T(8,128)(2,1)S(1)}, u32[]{:S(2)}, u32[]{:S(2)}) collective-permute-start(bf16[320,256]{1,0:T(8,128)(2,1)S(1)} %pad_maximum_fusion.2), channel_id=1, source_target_pairs={{0,4},{1,3},{2,6},{3,1},{4,0},{5,7},{6,2},{7,5},{8,12},{9,11},{10,... | collective-permute-start | bytes 491528 | tf_op jit(solution)/shard_map/ppermute | solution.py:193
  20.4 4.6 %collective-permute-done.1 = bf16[320,256]{1,0:T(8,128)(2,1)S(1)} collective-permute-done((bf16[320,256]{1,0:T(8,128)(2,1)S(1)}, bf16[320,256]{1,0:T(8,128)(2,1)S(1)}, u32[]{:S(2)}, u32[]{:S(2)}) %collective-permute-start.1) | collective-permute-done | bytes 163872 | tf_op jit(solution)/shard_map/ppermute | solution.py:193
  25.0 1.7 %collective-permute-start.2 = (bf16[640,256]{1,0:T(8,128)(2,1)S(1)}, bf16[640,256]{1,0:T(8,128)(2,1)S(1)}, u32[]{:S(2)}, u32[]{:S(2)}) collective-permute-start(bf16[640,256]{1,0:T(8,128)(2,1)S(1)} %pad_maximum_fusion.1), channel_id=1, source_target_pairs={{0,2},{1,5},{2,0},{3,7},{4,6},{5,1},{6,4},{7,3},{8,10},{9,13},{10,... | collective-permute-start | bytes 983048 | tf_op jit(solution)/shard_map/ppermute | solution.py:193
  26.7 5.4 %collective-permute-done.2 = bf16[640,256]{1,0:T(8,128)(2,1)S(1)} collective-permute-done((bf16[640,256]{1,0:T(8,128)(2,1)S(1)}, bf16[640,256]{1,0:T(8,128)(2,1)S(1)}, u32[]{:S(2)}, u32[]{:S(2)}) %collective-permute-start.2) | collective-permute-done | bytes 327712 | tf_op jit(solution)/shard_map/ppermute | solution.py:193
  32.2 0.1 collective-permute-start.3
  32.3 0.1 add_xor_fusion
  32.4 0.1 add_xor_fusion.2
  32.4 0.1 add_xor_fusion.1
  32.5 0.1 pad_add_fusion.2.where_ref
  32.6 1.7 %collective-permute-done.3.other_ref = bf16[1280,256]{1,0:T(8,128)(2,1)S(1)} collective-permute-done((bf16[1280,256]{1,0:T(8,128)(2,1)S(1)}, bf16[1280,256]{1,0:T(8,128)(2,1)S(1)}, u32[]{:S(2)}, u32[]{:S(2)}) %collective-permute-start.3) | collective-permute-done | bytes 655392 | tf_op jit(solution)/shard_map/ppermute | solution.py:197
  34.3 0.0 copy-done.5
  34.3 10.5 %sums.1 = (f32[16,8,4096]{2,1,0:T(8,128)}, f32[8,256]{1,0:T(8,128)}) custom-call(s32[18]{0:T(128)S(1)} %pad_add_fusion.2.where_ref, s32[9]{0:T(128)S(1)} %copy-done.5, bf16[1280,256]{1,0:T(8,128)(2,1)S(1)} %pad_maximum_fusion.own_ref, bf16[1280,256]{1,0:T(8,128)(2,1)S(1)} %collective-permute-done.3.other_ref), custom_call_target="tpu_custom_call" | custom-call | tf_op jit(solution)/shard_map/sums/pallas_call | solution.py:207
  (5 shorter events, 0.1 us)
Async XLA Ops:
  0.6 2.0 %copy-start = (bf16[256,7168]{1,0:T(8,128)(2,1)S(1)}, bf16[256,7168]{1,0:T(8,128)(2,1)}, u32[]{:S(2)}) copy-start(bf16[256,7168]{1,0:T(8,128)(2,1)} %x_hbm.1) | copy-start | bytes 11010052
  2.7 1.5 %copy-start.1 = (bf16[7168,128]{1,0:T(8,128)(2,1)S(1)}, bf16[7168,128]{1,0:T(8,128)(2,1)}, u32[]{:S(2)}) copy-start(bf16[7168,128]{1,0:T(8,128)(2,1)} %p_hbm.1) | copy-start | bytes 5505028
  4.2 0.7 %copy-start.2 = (f32[256,8]{0,1:T(8,128)S(1)}, f32[256,8]{0,1:T(8,128)}, u32[]{:S(2)}) copy-start(f32[256,8]{0,1:T(8,128)} %param.8) | copy-start | bytes 24580
  4.9 0.7 %copy-start.3 = (s32[256,8]{0,1:T(8,128)S(1)}, s32[256,8]{0,1:T(8,128)}, u32[]{:S(2)}) copy-start(s32[256,8]{0,1:T(8,128)} %param.9) | copy-start | bytes 24580
  5.6 0.7 %copy-start.4 = (s32[9]{0:T(128)S(1)}, s32[9]{0:T(128)}, u32[]{:S(2)}) copy-start(s32[9]{0:T(128)} %offsets_ref.3) | copy-start | bytes 112
  11.3 23.1 %copy-start.5 = (s32[9]{0:T(128)S(1)}, s32[9]{0:T(128)}, u32[]{:S(2)}) copy-start(s32[9]{0:T(128)} %offsets_ref.3) | copy-start | bytes 112
  11.3 8.3 %collective-permute-start = (bf16[160,256]{1,0:T(8,128)(2,1)S(1)}, bf16[160,256]{1,0:T(8,128)(2,1)S(1)}, u32[]{:S(2)}, u32[]{:S(2)}) collective-permute-start(bf16[160,256]{1,0:T(8,128)(2,1)S(1)} %project.1), channel_id=1, source_target_pairs={{0,8},{1,9},{2,10},{3,11},{4,12},{5,13},{6,14},{7,15},{8,0},{9,1},... | collective-permute-start | bytes 245768 | tf_op jit(solution)/shard_map/ppermute | solution.py:193
  19.6 5.4 %collective-permute-start.1 = (bf16[320,256]{1,0:T(8,128)(2,1)S(1)}, bf16[320,256]{1,0:T(8,128)(2,1)S(1)}, u32[]{:S(2)}, u32[]{:S(2)}) collective-permute-start(bf16[320,256]{1,0:T(8,128)(2,1)S(1)} %pad_maximum_fusion.2), channel_id=1, source_target_pairs={{0,4},{1,3},{2,6},{3,1},{4,0},{5,7},{6,2},{7,5},{8,12},{9,11},{10,... | collective-permute-start | bytes 491528 | tf_op jit(solution)/shard_map/ppermute | solution.py:193
  25.0 7.1 %collective-permute-start.2 = (bf16[640,256]{1,0:T(8,128)(2,1)S(1)}, bf16[640,256]{1,0:T(8,128)(2,1)S(1)}, u32[]{:S(2)}, u32[]{:S(2)}) collective-permute-start(bf16[640,256]{1,0:T(8,128)(2,1)S(1)} %pad_maximum_fusion.1), channel_id=1, source_target_pairs={{0,2},{1,5},{2,0},{3,7},{4,6},{5,1},{6,4},{7,3},{8,10},{9,13},{10,... | collective-permute-start | bytes 983048 | tf_op jit(solution)/shard_map/ppermute | solution.py:193
  32.2 2.2 %collective-permute-start.3 = (bf16[1280,256]{1,0:T(8,128)(2,1)S(1)}, bf16[1280,256]{1,0:T(8,128)(2,1)S(1)}, u32[]{:S(2)}, u32[]{:S(2)}) collective-permute-start(bf16[1280,256]{1,0:T(8,128)(2,1)S(1)} %pad_maximum_fusion.own_ref), channel_id=1, source_target_pairs={{0,1},{1,0},{2,3},{3,2},{4,5},{5,4},{6,7},{7,6},{8,9},{9,8},{10,11... | collective-permute-start | bytes 1966088 | tf_op jit(solution)/shard_map/ppermute | solution.py:197

commit v2 on v1

v2 whole, which is shorter than its diff:
```python
import functools

import jax
import jax.numpy as jnp
from jax import lax
from jax.experimental import pallas as pl
from jax.experimental.pallas import tpu as pltpu
from jax.sharding import PartitionSpec as P

EXPERTS = 256
TOPK = 8
DOCS = 8
CHUNK = 3584
VMEM_LIMIT = 32 * 1024 * 1024


def doc_of(offsets_ref, start):
    doc = jnp.int32(0)
    for i in range(1, DOCS):
        doc = doc + (start >= offsets_ref[i]).astype(jnp.int32)
    return doc


def project_kernel(
    gates_hbm, ids_hbm, offsets_hbm, x_hbm, g_hbm, p_hbm, out_ref,
    gates_ref, ids_ref, offsets_ref, x_buf, g_buf, p_buf, rows_buf, x_sem, g_sem, p_sem, small_sem,
):
    tok, depth = x_hbm.shape
    rank = p_hbm.shape[1] // 2
    half = rank // 2
    chunks = depth // CHUNK
    small = (
        pltpu.make_async_copy(offsets_hbm, offsets_ref, small_sem.at[0]),
        pltpu.make_async_copy(gates_hbm, gates_ref, small_sem.at[1]),
        pltpu.make_async_copy(ids_hbm, ids_ref, small_sem.at[2]),
    )

    def copies(i):
        cols = pl.ds(i * CHUNK, CHUNK)
        return (
            pltpu.make_async_copy(p_hbm.at[cols, :], p_buf.at[cols, :], p_sem.at[i]),
            pltpu.make_async_copy(x_hbm.at[:, cols], x_buf.at[:, cols], x_sem.at[i]),
            pltpu.make_async_copy(g_hbm.at[:, cols], g_buf.at[:, cols], g_sem.at[i]),
        )

    for copy in copies(0) + small:
        copy.start()
    for i in range(1, chunks):
        for copy in copies(i):
            copy.start()
    for copy in small:
        copy.wait()
    gates = gates_ref[...]
    high = gates.astype(jnp.bfloat16).astype(jnp.float32)
    ids = ids_ref[...].astype(jnp.float32)
    out_ref[2 * rank : 2 * rank + 16, :] = jnp.concatenate([ids, high], axis=0).astype(jnp.bfloat16)
    out_ref[2 * rank + 16 :, :] = jnp.concatenate(
        [gates - high, jnp.zeros_like(gates)], axis=0
    ).astype(jnp.bfloat16)
    start = lax.axis_index("ctx").astype(jnp.int32) * tok
    first = doc_of(offsets_ref, start)
    second = jnp.minimum(first + 1, DOCS - 1)
    position = start + lax.broadcasted_iota(jnp.int32, (1, tok), 1)
    length = jnp.where(
        position < offsets_ref[first + 1],
        offsets_ref[first + 1] - offsets_ref[first],
        offsets_ref[second + 1] - offsets_ref[second],
    ).astype(jnp.float32)
    scale = lax.rsqrt(length)
    a = jnp.zeros((tok, rank), jnp.float32)
    b = jnp.zeros((tok, rank), jnp.float32)
    for i in range(chunks):
        for copy in copies(i)[:2]:
            copy.wait()
        cols = pl.ds(i * CHUNK, CHUNK)
        p = p_buf[cols, :]
        a = a + jnp.dot(x_buf[:, cols], p, preferred_element_type=jnp.float32)[:, :rank]
        copies(i)[2].wait()
        b = b + jnp.dot(g_buf[:, cols], p, preferred_element_type=jnp.float32)[:, rank:]
    both = jnp.concatenate([a, b], axis=1).T
    out_ref[:rank, :] = both[:rank, :].astype(jnp.bfloat16)
    scaled = both[rank:, :] * scale
    for j in range(tok // 128):
        lanes = slice(j * 128, (j + 1) * 128)
        rows_buf[j, :, :] = scaled[:, lanes]
        for odd in range(2):
            picked = rows_buf[j, pl.ds(odd, half, stride=2), :]
            place = rank + odd * half
            out_ref[place : place + half, lanes] = picked.astype(jnp.bfloat16)


def add_block(shape, offsets_ref, ref, base, source, me, acc):
    experts, rank = shape
    half = rank // 2
    tok = ref.shape[1]
    start = source * tok
    first = doc_of(offsets_ref, start)
    position = start + lax.broadcasted_iota(jnp.int32, (1, tok), 1)
    in_first = (position < offsets_ref[first + 1]).astype(jnp.float32)
    a = ref[pl.ds(base, rank), :].astype(jnp.float32)
    b = ref[pl.ds(base + rank, rank), :].astype(jnp.float32)
    named = ref[pl.ds(base + 2 * rank, 16), :].astype(jnp.float32)
    low = ref[pl.ds(base + 2 * rank + 16, 16), :].astype(jnp.float32)
    ids, gates = named[:8, :], (named[8:, :] + low[:8, :]) * (EXPERTS / TOPK) ** 0.5
    even, odd = b[:half, :], b[half:, :]
    left = []
    for e in range(experts):
        mine = (me * experts + e).astype(jnp.float32)
        w = jnp.sum(jnp.where(ids == mine, gates, 0.0), axis=0, keepdims=True)
        left.append(jnp.concatenate([w * even, w * odd], axis=1).astype(jnp.bfloat16))
    left.append(jnp.concatenate([even, odd], axis=1).astype(jnp.bfloat16))
    left = jnp.concatenate(left, axis=0)
    a_first = a * in_first
    a_second = (a - a_first).astype(jnp.bfloat16)
    a_first = a_first.astype(jnp.bfloat16)
    none = jnp.zeros_like(a_first)
    right = jnp.concatenate(
        [
            jnp.concatenate([a_first, none], axis=1),
            jnp.concatenate([none, a_first], axis=1),
            jnp.concatenate([a_second, none], axis=1),
            jnp.concatenate([none, a_second], axis=1),
        ],
        axis=0,
    )
    both = lax.dot_general(
        left, right, (((1,), (1,)), ((), ())), preferred_element_type=jnp.float32
    )
    acc[first, :, :] += both[:, : 2 * rank]
    acc[jnp.minimum(first + 1, DOCS - 1), :, :] += both[:, 2 * rank :]


def add_all(shape, order, blocks, height, offsets_ref, refs, acc):
    me = lax.axis_index("ctx").astype(jnp.int32)
    stages = len(order[0])

    def source(slot, tag, flip):
        origin = me ^ flip
        path = slot | tag
        for k in range(stages):
            hop = jnp.where((origin & 1) == 1, order[1][k], order[0][k])
            origin = origin ^ (((path >> k) & 1) * hop)
        return origin

    slots = refs[0].shape[0] // height
    if slots <= 4:
        for ref, (tag, flip) in zip(refs, blocks):
            for s in range(slots):
                add_block(shape, offsets_ref, ref, s * height, source(s, tag, flip), me, acc)
        return

    def step(s, _):
        base = pl.multiple_of(s * height, height)
        for ref, (tag, flip) in zip(refs, blocks):
            add_block(shape, offsets_ref, ref, base, source(s, tag, flip), me, acc)
        return 0

    lax.fori_loop(0, slots, step, 0)


def first_kernel(shape, order, blocks, height, offsets_ref, *refs):
    acc = refs[-1]
    acc[...] = jnp.zeros_like(acc)
    add_all(shape, order, blocks, height, offsets_ref, refs[:-1], acc)


def next_kernel(shape, order, blocks, height, offsets_ref, held, *refs):
    add_all(shape, order, blocks, height, offsets_ref, refs[:-1], refs[-1])


def last_kernel(shape, order, blocks, height, offsets_ref, held, *refs):
    experts, rank = shape
    half = rank // 2
    refs, (routed_hbm, shared_ref, acc, sem) = refs[:-4], refs[-4:]
    add_all(shape, order, blocks, height, offsets_ref, refs, acc)
    copies = [
        pltpu.make_async_copy(
            acc.at[d, pl.ds(0, experts * half), :], routed_hbm.at[:, d, :], sem.at[d]
        )
        for d in range(DOCS)
    ]
    for copy in copies:
        copy.start()
    me = lax.axis_index("ctx").astype(jnp.int32)
    columns = rank * rank * experts // EXPERTS
    place = experts * half + me * columns // 128
    for j in range(shared_ref.shape[1] // 128):
        for d in range(DOCS):
            shared_ref[d : d + 1, j * 128 : (j + 1) * 128] = acc[d, pl.ds(place + j, 1), :]
    for copy in copies:
        copy.wait()


def on_device(devices, inputs, out_grads, gates, expert_ids, offsets, projections):
    tok, _ = inputs.shape
    rank = projections.shape[1] // 2
    half = rank // 2
    experts = EXPERTS // devices
    height = 2 * rank + 32
    smem = pl.BlockSpec(memory_space=pltpu.SMEM)
    vmem = pl.BlockSpec(memory_space=pltpu.VMEM)
    hbm = pl.BlockSpec(memory_space=pltpu.HBM)
    chunks = inputs.shape[1] // CHUNK
    params = pltpu.CompilerParams(vmem_limit_bytes=VMEM_LIMIT)

    def in_place(x):
        return pltpu.with_memory_space_constraint(x, pltpu.HBM)

    payload = pl.pallas_call(
        project_kernel,
        out_shape=pltpu.VMEM((height, tok), jnp.bfloat16),
        in_specs=[hbm] * 6,
        out_specs=vmem,
        scratch_shapes=[
            pltpu.VMEM((TOPK, tok), jnp.float32),
            pltpu.VMEM((TOPK, tok), jnp.int32),
            pltpu.SMEM(offsets.shape, jnp.int32),
            pltpu.VMEM(inputs.shape, jnp.bfloat16),
            pltpu.VMEM(inputs.shape, jnp.bfloat16),
            pltpu.VMEM(projections.shape, jnp.bfloat16),
            pltpu.VMEM((tok // 128, rank, 128), jnp.float32),
            pltpu.SemaphoreType.DMA((chunks,)),
            pltpu.SemaphoreType.DMA((chunks,)),
            pltpu.SemaphoreType.DMA((chunks,)),
            pltpu.SemaphoreType.DMA((3,)),
        ],
        compiler_params=params,
        name="project",
    )(*(in_place(x) for x in (gates.T, expert_ids.T, offsets, inputs, out_grads, projections)))

    far = [1 << k for k in range(devices.bit_length() - 2, 0, -1)]
    order = (far, far[-1:] + far[:-1])
    last = len(far) - 1

    def swap(block, k):
        return lax.ppermute(block, "ctx", [(i, i ^ order[i & 1][k]) for i in range(devices)])

    def core(block):
        return lax.ppermute(block, "ctx", [(i, i ^ 1) for i in range(devices)])

    def after(block, acc):
        return lax.optimization_barrier((block, acc))

    shape = (experts, rank)
    rows = (experts + 1) * half
    sums = pltpu.VMEM((DOCS, rows, 2 * rank), jnp.float32)

    def add(name, blocks, acc=None):
        held = [] if acc is None else [acc]
        kernel = first_kernel if acc is None else next_kernel
        return pl.pallas_call(
            functools.partial(kernel, shape, order, [b[1:] for b in blocks], height),
            out_shape=sums,
            in_specs=[smem] + [vmem] * (len(blocks) + len(held)),
            out_specs=vmem,
            input_output_aliases={1: 0} if held else {},
            compiler_params=params,
            name=name,
        )(offsets, *held, *(b[0] for b in blocks))

    near = payload
    for k in range(last - 1):
        near = jnp.concatenate([near, swap(near, k)], axis=0)
    bits = (1 << (last - 1), 1 << last)
    both = bits[0] | bits[1]
    one = swap(near, last - 1)
    two = swap(near, last)
    near_core = core(near)
    acc = add("sums_near", [(near, 0, 0), (near_core, 0, 1)])
    one, acc = after(one, acc)
    three = swap(one, last)
    one_core, two_core = core(one), core(two)
    blocks = [(one, bits[0], 0), (one_core, bits[0], 1), (two, bits[1], 0), (two_core, bits[1], 1)]
    acc = add("sums_next", blocks, acc)
    three, acc = after(three, acc)
    three_core = core(three)
    acc = add("sums_three", [(three, both, 0)], acc)
    three_core, acc = after(three_core, acc)
    blocks = [(three_core, both, 1)]
    columns = rank * rank // devices
    routed, shared, _ = pl.pallas_call(
        functools.partial(last_kernel, shape, order, [b[1:] for b in blocks], height),
        out_shape=(
            jax.ShapeDtypeStruct((experts * half, DOCS, 2 * rank), jnp.float32),
            jax.ShapeDtypeStruct((DOCS, max(columns, 128)), jnp.float32),
            sums,
        ),
        in_specs=[smem] + [vmem] * (len(blocks) + 1),
        out_specs=(hbm, vmem, vmem),
        scratch_shapes=[pltpu.SemaphoreType.DMA((DOCS,))],
        input_output_aliases={1: 2},
        compiler_params=params,
        name="sums_last",
    )(offsets, acc, *(b[0] for b in blocks))
    routed = routed.reshape(experts, half, DOCS, 2 * rank).transpose(0, 2, 1, 3)
    routed = routed.reshape(experts, DOCS, rank * rank)
    if columns < 128:
        me = lax.axis_index("ctx")
        shared = lax.dynamic_slice_in_dim(shared, me * columns % 128, columns, 1)
    return shared, routed


def solution(mesh):
    placed = (
        P(("groups", "ctx"), None),
        P(("groups", "ctx"), None),
        P(("groups", "ctx"), None),
        P(("groups", "ctx"), None),
        P("groups"),
        P(),
    )
    return jax.shard_map(
        functools.partial(on_device, mesh.shape["ctx"]),
        mesh=mesh,
        in_specs=placed,
        out_specs=(P("groups", "ctx"), P("ctx", "groups", None)),
        check_vma=False,
    )
```

time: 45.1 us -> 31.2 us (0.69)
  waiting for transfers between devices: 15.9 us -> 5.47 us
  local copies, waits for them, and re-layouts: 5.58 us -> 0.01 us
  starting transfers between devices: 6.7 us -> 10.3 us
  Pallas kernels: 15.5 us -> 14.3 us
    ppermute x4 -> x8, waiting for transfers between devices: 15.9 us -> 5.47 us  [the longest x4 5.29 us: swap(): lax.ppermute(block, 'ctx', [(i, i ^ order[i & 1][k]) for i in range(devic...]
    unnamed x12 -> x2, local copies, waits for them, and re-layouts: 5.58 us -> 0.01 us
    ppermute x4 -> x8, starting transfers between devices: 6.7 us -> 10.3 us  [the longest x4 9.39 us: swap(): lax.ppermute(block, 'ctx', [(i, i ^ order[i & 1][k]) for i in range(devic...]
    pallas_call x2 -> x5, Pallas kernels: 15.5 us -> 14.3 us  [the longest x3 6.23 us: add(): pl.pallas_call(functools.partial(kernel, shape, order, [b[1:] for b in bl...]
  transfers between devices with their start and end apart: 4 -> 8, of which waited for: 4 -> 4; matrix products, arithmetic and copies ran while one was open for 1% -> 0% of each run, Pallas kernels for 0% -> 20%
where the time goes in v2:
time: 31.2 us; the launch traced here: 30.8 us
  Pallas kernels  14.3 us (46%)
  starting transfers between devices  10.3 us (33%)
  waiting for transfers between devices  5.47 us (18%)
  between operations  0.69 us (2%)
    ppermute x4, starting transfers between devices, swap(): lax.ppermute(block, 'ctx', [(i, i ^ order[i & 1][k]) for i in range(devic...  9.39 us
    pallas_call x3, Pallas kernels, add(): pl.pallas_call(functools.partial(kernel, shape, order, [b[1:] for b in bl...  6.23 us
    ppermute x4, waiting for transfers between devices, swap(): lax.ppermute(block, 'ctx', [(i, i ^ order[i & 1][k]) for i in range(devic...  5.29 us
    pallas_call x1, Pallas kernels, on_device(): pl.pallas_call(project_kernel, out_shape=pltpu.VMEM((height, tok), jnp.bf...  4.89 us
    pallas_call x1, Pallas kernels, on_device(): pl.pallas_call(functools.partial(last_kernel, shape, order, [b[1:] for b...  3.18 us
    ppermute x4, starting transfers between devices, core(): return lax.ppermute(block, 'ctx', [(i, i ^ 1) for i in range(devices)])  0.91 us
  transfers between devices with their start and end apart: 8, of which 4 were waited for; matrix products, arithmetic and copies ran while one was open for 0% of the time, Pallas kernels for 20%

profile of v2, /device:TPU:0, one launch (start us, length us, event | category | flops | bytes accessed | tf_op | source)
XLA Modules:
  0.0 30.8 jit_solution(1393111233824197630)
XLA Ops:
  0.6 0.0 copy-start
  0.6 4.9 %project.1 = bf16[160,256]{1,0:T(8,128)(2,1)S(1)} custom-call(f32[8,256]{1,0:T(8,128)} %bitcast.7, s32[8,256]{1,0:T(8,128)} %bitcast.8, s32[9]{0:T(128)} %offsets_ref.7, bf16[256,7168]{1,0:T(8,128)(2,1)} %x_hbm.1, bf16[256,7168]{1,0:T(8,128)(2,1)} %g_hbm.1, bf16[7168,128]{1,0:T(8,128)(2,1)} %p_hbm.1), custom_call_target="tpu_custom_call" | custom-call | tf_op jit(solution)/shard_map/project/pallas_call | solution.py:209
  5.5 4.1 %collective-permute-start = (bf16[160,256]{1,0:T(8,128)(2,1)S(1)}, bf16[160,256]{1,0:T(8,128)(2,1)S(1)}, u32[]{:S(2)}, u32[]{:S(2)}) collective-permute-start(bf16[160,256]{1,0:T(8,128)(2,1)S(1)} %project.1), channel_id=1, source_target_pairs={{0,8},{1,3},{2,10},{3,1},{4,12},{5,7},{6,14},{7,5},{8,0},{9,11},{1... | collective-permute-start | bytes 245768 | tf_op jit(solution)/shard_map/ppermute | solution.py:236
  9.6 2.4 %collective-permute-done = bf16[160,256]{1,0:T(8,128)(2,1)S(1)} collective-permute-done((bf16[160,256]{1,0:T(8,128)(2,1)S(1)}, bf16[160,256]{1,0:T(8,128)(2,1)S(1)}, u32[]{:S(2)}, u32[]{:S(2)}) %collective-permute-start) | collective-permute-done | bytes 81952 | tf_op jit(solution)/shard_map/ppermute | solution.py:236
  12.1 0.1 collective-permute-start.2
  12.2 2.0 %collective-permute-start.1 = (bf16[320,256]{1,0:T(8,128)(2,1)S(1)}, bf16[320,256]{1,0:T(8,128)(2,1)S(1)}, u32[]{:S(2)}, u32[]{:S(2)}) collective-permute-start(bf16[320,256]{1,0:T(8,128)(2,1)S(1)} %pad_maximum_fusion.refs_0_), channel_id=1, source_target_pairs={{0,4},{1,9},{2,6},{3,11},{4,0},{5,13},{6,2},{7,15},{8,12},{9,1},{1... | collective-permute-start | bytes 491528 | tf_op jit(solution)/shard_map/ppermute | solution.py:236
  14.1 1.5 %collective-permute-start.5 = (bf16[320,256]{1,0:T(8,128)(2,1)S(1)}, bf16[320,256]{1,0:T(8,128)(2,1)S(1)}, u32[]{:S(2)}, u32[]{:S(2)}) collective-permute-start(bf16[320,256]{1,0:T(8,128)(2,1)S(1)} %pad_maximum_fusion.refs_0_), channel_id=1, source_target_pairs={{0,2},{1,5},{2,0},{3,7},{4,6},{5,1},{6,4},{7,3},{8,10},{9,13},{10,... | collective-permute-start | bytes 491528 | tf_op jit(solution)/shard_map/ppermute | solution.py:236
  15.6 0.0 collective-permute-done.2.refs_1_
  15.6 0.0 copy-done
  15.6 1.9 %sums_near.1.held = f32[8,544,128]{2,1,0:T(8,128)S(1)} custom-call(s32[9]{0:T(128)S(1)} %copy-done, bf16[320,256]{1,0:T(8,128)(2,1)S(1)} %pad_maximum_fusion.refs_0_, bf16[320,256]{1,0:T(8,128)(2,1)S(1)} %collective-permute-done.2.refs_1_), custom_call_target="tpu_custom_call" | custom-call | tf_op jit(solution)/shard_map/sums_near/pallas_call | solution.py:251
  17.6 2.5 %collective-permute-done.1.refs_0_ = bf16[320,256]{1,0:T(8,128)(2,1)S(1)} collective-permute-done((bf16[320,256]{1,0:T(8,128)(2,1)S(1)}, bf16[320,256]{1,0:T(8,128)(2,1)S(1)}, u32[]{:S(2)}, u32[]{:S(2)}) %collective-permute-start.1) | collective-permute-done | bytes 163872 | tf_op jit(solution)/shard_map/ppermute | solution.py:236
  20.0 0.0 collective-permute-done.5.refs_2_
  20.0 0.8 %collective-permute-start.6 = (bf16[320,256]{1,0:T(8,128)(2,1)S(1)}, bf16[320,256]{1,0:T(8,128)(2,1)S(1)}, u32[]{:S(2)}, u32[]{:S(2)}) collective-permute-start(bf16[320,256]{1,0:T(8,128)(2,1)S(1)} %collective-permute-done.5.refs_2_), channel_id=1, source_target_pairs={{0,1},{1,0},{2,3},{3,2},{4,5},{5,4},{6,7},{7,6},{8,9},{9,8},{10,11... | collective-permute-start | bytes 491528 | tf_op jit(solution)/shard_map/ppermute | solution.py:239
  20.9 0.0 collective-permute-start.4
  20.9 1.8 %collective-permute-start.3 = (bf16[320,256]{1,0:T(8,128)(2,1)S(1)}, bf16[320,256]{1,0:T(8,128)(2,1)S(1)}, u32[]{:S(2)}, u32[]{:S(2)}) collective-permute-start(bf16[320,256]{1,0:T(8,128)(2,1)S(1)} %collective-permute-done.1.refs_0_), channel_id=1, source_target_pairs={{0,2},{1,5},{2,0},{3,7},{4,6},{5,1},{6,4},{7,3},{8,10},{9,13},{10,... | collective-permute-start | bytes 491528 | tf_op jit(solution)/shard_map/ppermute | solution.py:236
  22.7 0.0 collective-permute-done.6.refs_3_
  22.7 0.0 collective-permute-done.4.refs_1_
  22.7 3.1 %sums_next.1.held = f32[8,544,128]{2,1,0:T(8,128)S(1)} custom-call(s32[9]{0:T(128)S(1)} %copy-done, f32[8,544,128]{2,1,0:T(8,128)S(1)} %sums_near.1.held, bf16[320,256]{1,0:T(8,128)(2,1)S(1)} %collective-permute-done.1.refs_0_, bf16[320,256]{1,0:T(8,128)(2,1)S(1)} %collective-permute-done.4.refs_1_, ...), custom_call_target="tpu_custom_call", output_to_operand_aliasing={{}: (1, {})} | custom-call | tf_op jit(solution)/shard_map/sums_next/pallas_call | solution.py:251
  25.8 0.4 %collective-permute-done.3.refs_0_ = bf16[320,256]{1,0:T(8,128)(2,1)S(1)} collective-permute-done((bf16[320,256]{1,0:T(8,128)(2,1)S(1)}, bf16[320,256]{1,0:T(8,128)(2,1)S(1)}, u32[]{:S(2)}, u32[]{:S(2)}) %collective-permute-start.3) | collective-permute-done | bytes 163872 | tf_op jit(solution)/shard_map/ppermute | solution.py:236
  26.2 0.0 collective-permute-start.7
  26.2 1.2 %sums_three.1.held = f32[8,544,128]{2,1,0:T(8,128)S(1)} custom-call(s32[9]{0:T(128)S(1)} %copy-done, f32[8,544,128]{2,1,0:T(8,128)S(1)} %sums_next.1.held, bf16[320,256]{1,0:T(8,128)(2,1)S(1)} %collective-permute-done.3.refs_0_), custom_call_target="tpu_custom_call", output_to_operand_aliasing={{}: (1, {})} | custom-call | tf_op jit(solution)/shard_map/sums_three/pallas_call | solution.py:251
  27.4 0.2 collective-permute-done.7.refs_0_
  27.6 3.2 %sums_last.1 = (f32[512,8,128]{2,1,0:T(8,128)}, f32[8,256]{1,0:T(8,128)}, f32[8,544,128]{2,1,0:T(8,128)S(1)}) custom-call(s32[9]{0:T(128)S(1)} %copy-done, f32[8,544,128]{2,1,0:T(8,128)S(1)} %sums_three.1.held, bf16[320,256]{1,0:T(8,128)(2,1)S(1)} %collective-permute-done.7.refs_0_), custom_call_target="tpu_custom_call", output_to_operand_aliasing={{2}: (1, {})} | custom-call | tf_op jit(solution)/shard_map/sums_last/pallas_call | solution.py:281
  (1 shorter events, 0.0 us)
Async XLA Ops:
  0.6 15.0 %copy-start = (s32[9]{0:T(128)S(1)}, s32[9]{0:T(128)}, u32[]{:S(2)}) copy-start(s32[9]{0:T(128)} %offsets_ref.7) | copy-start | bytes 112
  5.5 6.5 %collective-permute-start = (bf16[160,256]{1,0:T(8,128)(2,1)S(1)}, bf16[160,256]{1,0:T(8,128)(2,1)S(1)}, u32[]{:S(2)}, u32[]{:S(2)}) collective-permute-start(bf16[160,256]{1,0:T(8,128)(2,1)S(1)} %project.1), channel_id=1, source_target_pairs={{0,8},{1,3},{2,10},{3,1},{4,12},{5,7},{6,14},{7,5},{8,0},{9,11},{1... | collective-permute-start | bytes 245768 | tf_op jit(solution)/shard_map/ppermute | solution.py:236
  12.1 3.6 %collective-permute-start.2 = (bf16[320,256]{1,0:T(8,128)(2,1)S(1)}, bf16[320,256]{1,0:T(8,128)(2,1)S(1)}, u32[]{:S(2)}, u32[]{:S(2)}) collective-permute-start(bf16[320,256]{1,0:T(8,128)(2,1)S(1)} %pad_maximum_fusion.refs_0_), channel_id=1, source_target_pairs={{0,1},{1,0},{2,3},{3,2},{4,5},{5,4},{6,7},{7,6},{8,9},{9,8},{10,11... | collective-permute-start | bytes 491528 | tf_op jit(solution)/shard_map/ppermute | solution.py:239
  12.2 7.9 %collective-permute-start.1 = (bf16[320,256]{1,0:T(8,128)(2,1)S(1)}, bf16[320,256]{1,0:T(8,128)(2,1)S(1)}, u32[]{:S(2)}, u32[]{:S(2)}) collective-permute-start(bf16[320,256]{1,0:T(8,128)(2,1)S(1)} %pad_maximum_fusion.refs_0_), channel_id=1, source_target_pairs={{0,4},{1,9},{2,6},{3,11},{4,0},{5,13},{6,2},{7,15},{8,12},{9,1},{1... | collective-permute-start | bytes 491528 | tf_op jit(solution)/shard_map/ppermute | solution.py:236
  14.1 5.9 %collective-permute-start.5 = (bf16[320,256]{1,0:T(8,128)(2,1)S(1)}, bf16[320,256]{1,0:T(8,128)(2,1)S(1)}, u32[]{:S(2)}, u32[]{:S(2)}) collective-permute-start(bf16[320,256]{1,0:T(8,128)(2,1)S(1)} %pad_maximum_fusion.refs_0_), channel_id=1, source_target_pairs={{0,2},{1,5},{2,0},{3,7},{4,6},{5,1},{6,4},{7,3},{8,10},{9,13},{10,... | collective-permute-start | bytes 491528 | tf_op jit(solution)/shard_map/ppermute | solution.py:236
  20.0 2.7 %collective-permute-start.6 = (bf16[320,256]{1,0:T(8,128)(2,1)S(1)}, bf16[320,256]{1,0:T(8,128)(2,1)S(1)}, u32[]{:S(2)}, u32[]{:S(2)}) collective-permute-start(bf16[320,256]{1,0:T(8,128)(2,1)S(1)} %collective-permute-done.5.refs_2_), channel_id=1, source_target_pairs={{0,1},{1,0},{2,3},{3,2},{4,5},{5,4},{6,7},{7,6},{8,9},{9,8},{10,11... | collective-permute-start | bytes 491528 | tf_op jit(solution)/shard_map/ppermute | solution.py:239
  20.9 1.8 %collective-permute-start.4 = (bf16[320,256]{1,0:T(8,128)(2,1)S(1)}, bf16[320,256]{1,0:T(8,128)(2,1)S(1)}, u32[]{:S(2)}, u32[]{:S(2)}) collective-permute-start(bf16[320,256]{1,0:T(8,128)(2,1)S(1)} %collective-permute-done.1.refs_0_), channel_id=1, source_target_pairs={{0,1},{1,0},{2,3},{3,2},{4,5},{5,4},{6,7},{7,6},{8,9},{9,8},{10,11... | collective-permute-start | bytes 491528 | tf_op jit(solution)/shard_map/ppermute | solution.py:239
  20.9 5.3 %collective-permute-start.3 = (bf16[320,256]{1,0:T(8,128)(2,1)S(1)}, bf16[320,256]{1,0:T(8,128)(2,1)S(1)}, u32[]{:S(2)}, u32[]{:S(2)}) collective-permute-start(bf16[320,256]{1,0:T(8,128)(2,1)S(1)} %collective-permute-done.1.refs_0_), channel_id=1, source_target_pairs={{0,2},{1,5},{2,0},{3,7},{4,6},{5,1},{6,4},{7,3},{8,10},{9,13},{10,... | collective-permute-start | bytes 491528 | tf_op jit(solution)/shard_map/ppermute | solution.py:236
  26.2 1.4 %collective-permute-start.7 = (bf16[320,256]{1,0:T(8,128)(2,1)S(1)}, bf16[320,256]{1,0:T(8,128)(2,1)S(1)}, u32[]{:S(2)}, u32[]{:S(2)}) collective-permute-start(bf16[320,256]{1,0:T(8,128)(2,1)S(1)} %collective-permute-done.3.refs_0_), channel_id=1, source_target_pairs={{0,1},{1,0},{2,3},{3,2},{4,5},{5,4},{6,7},{7,6},{8,9},{9,8},{10,11... | collective-permute-start | bytes 491528 | tf_op jit(solution)/shard_map/ppermute | solution.py:239

commit v3 on v2

--- a/solution.py
+++ b/solution.py
@@ -11,6 +11,7 @@
 TOPK = 8
 DOCS = 8
 CHUNK = 3584
+FLUSH = 2
 VMEM_LIMIT = 32 * 1024 * 1024
 
 
@@ -22,8 +23,8 @@
 
 
 def project_kernel(
-    gates_hbm, ids_hbm, offsets_hbm, x_hbm, g_hbm, p_hbm, out_ref,
-    gates_ref, ids_ref, offsets_ref, x_buf, g_buf, p_buf, rows_buf, x_sem, g_sem, p_sem, small_sem,
+    gates_hbm, ids_hbm, offsets_hbm, x_hbm, g_hbm, p_hbm, out_ref, offsets_ref,
+    gates_ref, ids_ref, x_buf, g_buf, p_buf, rows_buf, x_sem, g_sem, p_sem, small_sem,
 ):
     tok, depth = x_hbm.shape
     rank = p_hbm.shape[1] // 2
@@ -89,8 +90,8 @@
             out_ref[place : place + half, lanes] = picked.astype(jnp.bfloat16)
 
 
-def add_block(shape, offsets_ref, ref, base, source, me, acc):
-    experts, rank = shape
+def prepare(shape, offsets_ref, ref, base, source):
+    rank = shape[1]
     half = rank // 2
     tok = ref.shape[1]
     start = source * tok
@@ -102,14 +103,6 @@
     named = ref[pl.ds(base + 2 * rank, 16), :].astype(jnp.float32)
     low = ref[pl.ds(base + 2 * rank + 16, 16), :].astype(jnp.float32)
     ids, gates = named[:8, :], (named[8:, :] + low[:8, :]) * (EXPERTS / TOPK) ** 0.5
-    even, odd = b[:half, :], b[half:, :]
-    left = []
-    for e in range(experts):
-        mine = (me * experts + e).astype(jnp.float32)
-        w = jnp.sum(jnp.where(ids == mine, gates, 0.0), axis=0, keepdims=True)
-        left.append(jnp.concatenate([w * even, w * odd], axis=1).astype(jnp.bfloat16))
-    left.append(jnp.concatenate([even, odd], axis=1).astype(jnp.bfloat16))
-    left = jnp.concatenate(left, axis=0)
     a_first = a * in_first
     a_second = (a - a_first).astype(jnp.bfloat16)
     a_first = a_first.astype(jnp.bfloat16)
@@ -123,70 +116,113 @@
         ],
         axis=0,
     )
+    docs = first, jnp.minimum(first + 1, DOCS - 1)
+    return docs, ids, gates, b[:half, :], b[half:, :], right
+
+
+def add_block(shape, block, me, acc, again, begin=0, end=None):
+    experts, rank = shape
+    half = rank // 2
+    (first, second), ids, gates, even, odd, right = block
+    end = experts + 1 if end is None else end
+    left = []
+    for e in range(begin, end):
+        if e == experts:
+            left.append(jnp.concatenate([even, odd], axis=1).astype(jnp.bfloat16))
+            continue
+        mine = (me * experts + e).astype(jnp.float32)
+        w = jnp.sum(jnp.where(ids == mine, gates, 0.0), axis=0, keepdims=True)
+        left.append(jnp.concatenate([w * even, w * odd], axis=1).astype(jnp.bfloat16))
+    left = jnp.concatenate(left, axis=0)
     both = lax.dot_general(
         left, right, (((1,), (1,)), ((), ())), preferred_element_type=jnp.float32
     )
-    acc[first, :, :] += both[:, : 2 * rank]
-    acc[jnp.minimum(first + 1, DOCS - 1), :, :] += both[:, 2 * rank :]
-
-
-def add_all(shape, order, blocks, height, offsets_ref, refs, acc):
+    rows = pl.ds(begin * half, (end - begin) * half)
+    acc[first, rows, :] += both[:, : 2 * rank]
+    again[second, rows, :] += both[:, 2 * rank :]
+
+
+def origin_of(order, me, slot, tag, flip):
+    origin = me ^ flip
+    path = slot | tag
+    for k in range(len(order[0])):
+        hop = jnp.where((origin & 1) == 1, order[1][k], order[0][k])
+        origin = origin ^ (((path >> k) & 1) * hop)
+    return origin
+
+
+def add_all(shape, order, blocks, height, offsets_ref, refs, acc, again):
     me = lax.axis_index("ctx").astype(jnp.int32)
-    stages = len(order[0])
-
-    def source(slot, tag, flip):
-        origin = me ^ flip
-        path = slot | tag
-        for k in range(stages):
-            hop = jnp.where((origin & 1) == 1, order[1][k], order[0][k])
-            origin = origin ^ (((path >> k) & 1) * hop)
-        return origin
-
     slots = refs[0].shape[0] // height
+
+    def add(ref, s, base, tag, flip):
+        source = origin_of(order, me, s, tag, flip)
+        add_block(shape, prepare(shape, offsets_ref, ref, base, source), me, acc, again)
+
     if slots <= 4:
         for ref, (tag, flip) in zip(refs, blocks):
             for s in range(slots):
-                add_block(shape, offsets_ref, ref, s * height, source(s, tag, flip), me, acc)
+                add(ref, s, s * height, tag, flip)
         return
 
     def step(s, _):
-        base = pl.multiple_of(s * height, height)
         for ref, (tag, flip) in zip(refs, blocks):
-            add_block(shape, offsets_ref, ref, base, source(s, tag, flip), me, acc)
+            add(ref, s, pl.multiple_of(s * height, height), tag, flip)
         return 0
 
     lax.fori_loop(0, slots, step, 0)
 
 
 def first_kernel(shape, order, blocks, height, offsets_ref, *refs):
-    acc = refs[-1]
+    refs, (acc, again) = refs[:-2], refs[-2:]
     acc[...] = jnp.zeros_like(acc)
-    add_all(shape, order, blocks, height, offsets_ref, refs[:-1], acc)
-
-
-def next_kernel(shape, order, blocks, height, offsets_ref, held, *refs):
-    add_all(shape, order, blocks, height, offsets_ref, refs[:-1], refs[-1])
+    again[...] = jnp.zeros_like(again)
+    add_all(shape, order, blocks, height, offsets_ref, refs, acc, again)
+
+
+def next_kernel(shape, order, blocks, height, offsets_ref, acc_in, again_in, *refs):
+    add_all(shape, order, blocks, height, offsets_ref, refs[:-2], *refs[-2:])
+
+
+def fold_kernel(shape, order, blocks, height, offsets_ref, acc_in, again, *refs):
+    refs, acc = refs[:-1], refs[-1]
+    add_all(shape, order, blocks, height, offsets_ref, refs, acc, again)
+    acc[...] += again[...]
 
 
 def last_kernel(shape, order, blocks, height, offsets_ref, held, *refs):
     experts, rank = shape
     half = rank // 2
-    refs, (routed_hbm, shared_ref, acc, sem) = refs[:-4], refs[-4:]
-    add_all(shape, order, blocks, height, offsets_ref, refs, acc)
-    copies = [
-        pltpu.make_async_copy(
-            acc.at[d, pl.ds(0, experts * half), :], routed_hbm.at[:, d, :], sem.at[d]
-        )
-        for d in range(DOCS)
-    ]
-    for copy in copies:
-        copy.start()
+    refs, (routed_hbm, shared_hbm, acc, shared_buf, sem) = refs[:-5], refs[-5:]
     me = lax.axis_index("ctx").astype(jnp.int32)
+    slots = refs[0].shape[0] // height
+    if slots <= 4:
+        ready = [
+            prepare(shape, offsets_ref, ref, s * height, origin_of(order, me, s, tag, flip))
+            for ref, (tag, flip) in zip(refs, blocks)
+            for s in range(slots)
+        ]
+    else:
+        ready = []
+        add_all(shape, order, blocks, height, offsets_ref, refs, acc, acc)
+    cuts = [experts * k // FLUSH for k in range(FLUSH + 1)]
+    copies = []
+    for k in range(FLUSH):
+        for block in ready:
+            add_block(shape, block, me, acc, acc, cuts[k], cuts[k + 1] + (k == FLUSH - 1))
+        rows = pl.ds(cuts[k] * half, (cuts[k + 1] - cuts[k]) * half)
+        for d in range(DOCS):
+            copies.append(
+                pltpu.make_async_copy(acc.at[d, rows, :], routed_hbm.at[rows, d, :], sem.at[k, d])
+            )
+            copies[-1].start()
     columns = rank * rank * experts // EXPERTS
     place = experts * half + me * columns // 128
-    for j in range(shared_ref.shape[1] // 128):
+    for j in range(shared_buf.shape[1] // 128):
         for d in range(DOCS):
-            shared_ref[d : d + 1, j * 128 : (j + 1) * 128] = acc[d, pl.ds(place + j, 1), :]
+            shared_buf[d : d + 1, j * 128 : (j + 1) * 128] = acc[d, pl.ds(place + j, 1), :]
+    copies.append(pltpu.make_async_copy(shared_buf, shared_hbm, sem.at[FLUSH, 0]))
+    copies[-1].start()
     for copy in copies:
         copy.wait()
 
@@ -206,15 +242,17 @@
     def in_place(x):
         return pltpu.with_memory_space_constraint(x, pltpu.HBM)
 
-    payload = pl.pallas_call(
+    payload, offsets = pl.pallas_call(
         project_kernel,
-        out_shape=pltpu.VMEM((height, tok), jnp.bfloat16),
+        out_shape=(
+            pltpu.VMEM((height, tok), jnp.bfloat16),
+            pltpu.SMEM(offsets.shape, jnp.int32),
+        ),
         in_specs=[hbm] * 6,
-        out_specs=vmem,
+        out_specs=(vmem, smem),
         scratch_shapes=[
             pltpu.VMEM((TOPK, tok), jnp.float32),
             pltpu.VMEM((TOPK, tok), jnp.int32),
-            pltpu.SMEM(offsets.shape, jnp.int32),
             pltpu.VMEM(inputs.shape, jnp.bfloat16),
             pltpu.VMEM(inputs.shape, jnp.bfloat16),
             pltpu.VMEM(projections.shape, jnp.bfloat16),
@@ -229,7 +267,7 @@
     )(*(in_place(x) for x in (gates.T, expert_ids.T, offsets, inputs, out_grads, projections)))
 
     far = [1 << k for k in range(devices.bit_length() - 2, 0, -1)]
-    order = (far, far[-1:] + far[:-1])
+    order = (far[:1] + far[-1:] + far[1:-1], far[1:-1] + far[:1] + far[-1:])
     last = len(far) - 1
 
     def swap(block, k):
@@ -245,36 +283,42 @@
     rows = (experts + 1) * half
     sums = pltpu.VMEM((DOCS, rows, 2 * rank), jnp.float32)
 
-    def add(name, blocks, acc=None):
-        held = [] if acc is None else [acc]
-        kernel = first_kernel if acc is None else next_kernel
+    def add(name, blocks, acc=(), fold=False):
+        kernel = fold_kernel if fold else next_kernel if acc else first_kernel
         return pl.pallas_call(
             functools.partial(kernel, shape, order, [b[1:] for b in blocks], height),
-            out_shape=sums,
-            in_specs=[smem] + [vmem] * (len(blocks) + len(held)),
-            out_specs=vmem,
-            input_output_aliases={1: 0} if held else {},
+            out_shape=sums if fold else (sums, sums),
+            in_specs=[smem] + [vmem] * (len(blocks) + len(acc)),
+            out_specs=vmem if fold else (vmem, vmem),
+            input_output_aliases={1: 0} if fold else {1: 0, 2: 1} if acc else {},
             compiler_params=params,
             name=name,
-        )(offsets, *held, *(b[0] for b in blocks))
+        )(offsets, *acc, *(b[0] for b in blocks))
 
     near = payload
+    acc = add("sums_own", [(payload, 0, 0)])
     for k in range(last - 1):
-        near = jnp.concatenate([near, swap(near, k)], axis=0)
+        got = swap(near, k)
+        got, acc = after(got, acc)
+        near = jnp.concatenate([near, got], axis=0)
+        if k < last - 2:
+            acc = add("sums_got", [(got, 1 << k, 0)], acc)
     bits = (1 << (last - 1), 1 << last)
     both = bits[0] | bits[1]
     one = swap(near, last - 1)
+    acc = add("sums_got", [(got, 1 << (last - 2), 0)], acc)
+    near, acc = after(near, acc)
     two = swap(near, last)
     near_core = core(near)
-    acc = add("sums_near", [(near, 0, 0), (near_core, 0, 1)])
     one, acc = after(one, acc)
     three = swap(one, last)
+    acc = add("sums_next", [(one, bits[0], 0), (two, bits[1], 0), (near_core, 0, 1)], acc)
+    one, two, acc = lax.optimization_barrier((one, two, acc))
     one_core, two_core = core(one), core(two)
-    blocks = [(one, bits[0], 0), (one_core, bits[0], 1), (two, bits[1], 0), (two_core, bits[1], 1)]
-    acc = add("sums_next", blocks, acc)
     three, acc = after(three, acc)
     three_core = core(three)
-    acc = add("sums_three", [(three, both, 0)], acc)
+    blocks = [(three, both, 0), (one_core, bits[0], 1), (two_core, bits[1], 1)]
+    acc = add("sums_three", blocks, acc, fold=True)
     three_core, acc = after(three_core, acc)
     blocks = [(three_core, both, 1)]
     columns = rank * rank // devices
@@ -286,8 +330,11 @@
             sums,
         ),
         in_specs=[smem] + [vmem] * (len(blocks) + 1),
-        out_specs=(hbm, vmem, vmem),
-        scratch_shapes=[pltpu.SemaphoreType.DMA((DOCS,))],
+        out_specs=(hbm, hbm, vmem),
+        scratch_shapes=[
+            pltpu.VMEM((DOCS, max(columns, 128)), jnp.float32),
+            pltpu.SemaphoreType.DMA((FLUSH + 1, DOCS)),
+        ],
         input_output_aliases={1: 2},
         compiler_params=params,
         name="sums_last",

time: 31.2 us -> 28.4 us (0.910)
  the two profiles are of different devices: /device:TPU:0 before, /device:TPU:27 now
where the time goes in v3:
time: 28.4 us; the launch traced here: 28.2 us
  Pallas kernels  11.2 us (39%)
  starting transfers between devices  9.82 us (35%)
  waiting for transfers between devices  6.42 us (23%)
  between operations  0.69 us (2%)
    ppermute x4, starting transfers between devices, core(): return lax.ppermute(block, 'ctx', [(i, i ^ 1) for i in range(devices)])  8.07 us
    ppermute x4, waiting for transfers between devices, swap(): lax.ppermute(block, 'ctx', [(i, i ^ order[i & 1][k]) for i in range(devic...  6.41 us
    pallas_call x1, Pallas kernels, on_device(): pl.pallas_call(project_kernel, out_shape=(pltpu.VMEM((height, tok), jnp.b...  4.89 us
    pallas_call x4, Pallas kernels, add(): pl.pallas_call(functools.partial(kernel, shape, order, [b[1:] for b in bl...  4.36 us
    pallas_call x1, Pallas kernels, on_device(): pl.pallas_call(functools.partial(last_kernel, shape, order, [b[1:] for b...  1.99 us
    ppermute x4, starting transfers between devices, swap(): lax.ppermute(block, 'ctx', [(i, i ^ order[i & 1][k]) for i in range(devic...  1.75 us
  transfers between devices with their start and end apart: 8, of which 3 were waited for; matrix products, arithmetic and copies ran while one was open for 0% of the time, Pallas kernels for 15%

profile of v3, /device:TPU:27, one launch (start us, length us, event | category | flops | bytes accessed | tf_op | source)
XLA Modules:
  0.0 28.2 jit_solution(18007285921966845966)
XLA Ops:
  0.6 4.9 %project.1 = (bf16[160,256]{1,0:T(8,128)(2,1)S(1)}, s32[9]{0:T(128)S(4)}) custom-call(f32[8,256]{1,0:T(8,128)} %bitcast.7, s32[8,256]{1,0:T(8,128)} %bitcast.8, s32[9]{0:T(128)} %offsets_hbm.1, bf16[256,7168]{1,0:T(8,128)(2,1)} %x_hbm.1, bf16[256,7168]{1,0:T(8,128)(2,1)} %g_hbm.1, bf16[7168,128]{1,0:T(8,128)(2,1)} %p_hbm.1), custom_call_target="tpu_custom_call" | custom-call | tf_op jit(solution)/shard_map/project/pallas_call | solution.py:245
  5.5 0.2 collective-permute-start
  5.8 0.6 %sums_own.1 = (f32[8,544,128]{2,1,0:T(8,128)S(1)}, f32[8,544,128]{2,1,0:T(8,128)S(1)}) custom-call(s32[9]{0:T(128)S(4)} %get-tuple-element.30.offsets_ref, bf16[160,256]{1,0:T(8,128)(2,1)S(1)} %get-tuple-element.31.refs_0_), custom_call_target="tpu_custom_call" | custom-call | tf_op jit(solution)/shard_map/sums_own/pallas_call | solution.py:288
  6.4 2.5 %collective-permute-done.refs_0_ = bf16[160,256]{1,0:T(8,128)(2,1)S(1)} collective-permute-done((bf16[160,256]{1,0:T(8,128)(2,1)S(1)}, bf16[160,256]{1,0:T(8,128)(2,1)S(1)}, u32[]{:S(2)}, u32[]{:S(2)}) %collective-permute-start) | collective-permute-done | bytes 81952 | tf_op jit(solution)/shard_map/ppermute | solution.py:274
  8.9 0.1 collective-permute-start.1
  8.9 0.4 %sums_got.1 = (f32[8,544,128]{2,1,0:T(8,128)S(1)}, f32[8,544,128]{2,1,0:T(8,128)S(1)}) custom-call(s32[9]{0:T(128)S(4)} %get-tuple-element.30.offsets_ref, f32[8,544,128]{2,1,0:T(8,128)S(1)} %get-tuple-element.35.acc_in, f32[8,544,128]{2,1,0:T(8,128)S(1)} %get-tuple-element.36.again_in, ...), custom_call_target="tpu_custom_call", output_to_operand_aliasing={{0}: (1, {}), {1}: (2, {})} | custom-call | tf_op jit(solution)/shard_map/sums_got/pallas_call | solution.py:288
  9.3 4.0 %collective-permute-start.4 = (bf16[320,256]{1,0:T(8,128)(2,1)S(1)}, bf16[320,256]{1,0:T(8,128)(2,1)S(1)}, u32[]{:S(2)}, u32[]{:S(2)}) collective-permute-start(bf16[320,256]{1,0:T(8,128)(2,1)S(1)} %constant_dynamic-update-slice_fusion), channel_id=1, source_target_pairs={{0,1},{1,0},{2,3},{3,2},{4,5},{5,4},{6,7},{7,6},{8,9},{9,8},{10,11... | collective-permute-start | bytes 491528 | tf_op jit(solution)/shard_map/ppermute | solution.py:277
  13.4 1.2 %collective-permute-start.3 = (bf16[320,256]{1,0:T(8,128)(2,1)S(1)}, bf16[320,256]{1,0:T(8,128)(2,1)S(1)}, u32[]{:S(2)}, u32[]{:S(2)}) collective-permute-start(bf16[320,256]{1,0:T(8,128)(2,1)S(1)} %constant_dynamic-update-slice_fusion), channel_id=1, source_target_pairs={{0,4},{1,3},{2,6},{3,1},{4,0},{5,7},{6,2},{7,5},{8,12},{9,11},{10,... | collective-permute-start | bytes 491528 | tf_op jit(solution)/shard_map/ppermute | solution.py:274
  14.6 1.0 %collective-permute-done.1.refs_0_ = bf16[320,256]{1,0:T(8,128)(2,1)S(1)} collective-permute-done((bf16[320,256]{1,0:T(8,128)(2,1)S(1)}, bf16[320,256]{1,0:T(8,128)(2,1)S(1)}, u32[]{:S(2)}, u32[]{:S(2)}) %collective-permute-start.1) | collective-permute-done | bytes 163872 | tf_op jit(solution)/shard_map/ppermute | solution.py:274
  15.6 0.3 collective-permute-start.2
  15.9 0.0 collective-permute-done.4.refs_2_
  15.9 2.9 %collective-permute-done.3.refs_1_ = bf16[320,256]{1,0:T(8,128)(2,1)S(1)} collective-permute-done((bf16[320,256]{1,0:T(8,128)(2,1)S(1)}, bf16[320,256]{1,0:T(8,128)(2,1)S(1)}, u32[]{:S(2)}, u32[]{:S(2)}) %collective-permute-start.3) | collective-permute-done | bytes 163872 | tf_op jit(solution)/shard_map/ppermute | solution.py:274
  18.8 1.5 %sums_next.1 = (f32[8,544,128]{2,1,0:T(8,128)S(1)}, f32[8,544,128]{2,1,0:T(8,128)S(1)}) custom-call(s32[9]{0:T(128)S(4)} %get-tuple-element.30.offsets_ref, f32[8,544,128]{2,1,0:T(8,128)S(1)} %get-tuple-element.43.acc_in, f32[8,544,128]{2,1,0:T(8,128)S(1)} %get-tuple-element.44.again_in, ...), custom_call_target="tpu_custom_call", output_to_operand_aliasing={{0}: (1, {}), {1}: (2, {})} | custom-call | tf_op jit(solution)/shard_map/sums_next/pallas_call | solution.py:288
  20.3 0.3 %collective-permute-start.6 = (bf16[320,256]{1,0:T(8,128)(2,1)S(1)}, bf16[320,256]{1,0:T(8,128)(2,1)S(1)}, u32[]{:S(2)}, u32[]{:S(2)}) collective-permute-start(bf16[320,256]{1,0:T(8,128)(2,1)S(1)} %collective-permute-done.1.refs_0_), channel_id=1, source_target_pairs={{0,1},{1,0},{2,3},{3,2},{4,5},{5,4},{6,7},{7,6},{8,9},{9,8},{10,11... | collective-permute-start | bytes 491528 | tf_op jit(solution)/shard_map/ppermute | solution.py:277
  20.6 0.2 collective-permute-start.7
  20.9 0.0 collective-permute-done.2.refs_0_
  20.9 3.5 %collective-permute-start.5 = (bf16[320,256]{1,0:T(8,128)(2,1)S(1)}, bf16[320,256]{1,0:T(8,128)(2,1)S(1)}, u32[]{:S(2)}, u32[]{:S(2)}) collective-permute-start(bf16[320,256]{1,0:T(8,128)(2,1)S(1)} %collective-permute-done.2.refs_0_), channel_id=1, source_target_pairs={{0,1},{1,0},{2,3},{3,2},{4,5},{5,4},{6,7},{7,6},{8,9},{9,8},{10,11... | collective-permute-start | bytes 491528 | tf_op jit(solution)/shard_map/ppermute | solution.py:277
  24.3 0.0 collective-permute-done.6.refs_1_
  24.3 0.0 collective-permute-done.7.refs_2_
  24.3 1.9 %sums_three.1.held = f32[8,544,128]{2,1,0:T(8,128)S(1)} custom-call(s32[9]{0:T(128)S(4)} %get-tuple-element.30.offsets_ref, f32[8,544,128]{2,1,0:T(8,128)S(1)} %get-tuple-element.50.acc_in, f32[8,544,128]{2,1,0:T(8,128)S(1)} %get-tuple-element.51.again, bf16[320,256]{1,0:T(8,128)(2,1)S(1)} %collective-permute-done.2.refs_0_, ...), custom_call_target="tpu_custom_call", output_to_operand_aliasing={{}: (1, {})} | custom-call | tf_op jit(solution)/shard_map/sums_three/pallas_call | solution.py:288
  26.2 0.0 collective-permute-done.5.refs_0_
  26.2 2.0 %sums_last.1 = (f32[512,8,128]{2,1,0:T(8,128)}, f32[8,256]{1,0:T(8,128)}, f32[8,544,128]{2,1,0:T(8,128)S(1)}) custom-call(s32[9]{0:T(128)S(4)} %get-tuple-element.30.offsets_ref, f32[8,544,128]{2,1,0:T(8,128)S(1)} %sums_three.1.held, bf16[320,256]{1,0:T(8,128)(2,1)S(1)} %collective-permute-done.5.refs_0_), custom_call_target="tpu_custom_call", output_to_operand_aliasing={{2}: (1, {})} | custom-call | tf_op jit(solution)/shard_map/sums_last/pallas_call | solution.py:325
  (2 shorter events, 0.0 us)
Async XLA Ops:
  5.5 3.4 %collective-permute-start = (bf16[160,256]{1,0:T(8,128)(2,1)S(1)}, bf16[160,256]{1,0:T(8,128)(2,1)S(1)}, u32[]{:S(2)}, u32[]{:S(2)}) collective-permute-start(bf16[160,256]{1,0:T(8,128)(2,1)S(1)} %get-tuple-element.31.refs_0_), channel_id=1, source_target_pairs={{0,8},{1,5},{2,10},{3,7},{4,12},{5,1},{6,14},{7,3},{8,0},{9,13},{1... | collective-permute-start | bytes 245768 | tf_op jit(solution)/shard_map/ppermute | solution.py:274
  8.9 6.7 %collective-permute-start.1 = (bf16[320,256]{1,0:T(8,128)(2,1)S(1)}, bf16[320,256]{1,0:T(8,128)(2,1)S(1)}, u32[]{:S(2)}, u32[]{:S(2)}) collective-permute-start(bf16[320,256]{1,0:T(8,128)(2,1)S(1)} %constant_dynamic-update-slice_fusion), channel_id=1, source_target_pairs={{0,2},{1,9},{2,0},{3,11},{4,6},{5,13},{6,4},{7,15},{8,10},{9,1},{1... | collective-permute-start | bytes 491528 | tf_op jit(solution)/shard_map/ppermute | solution.py:274
  9.3 6.5 %collective-permute-start.4 = (bf16[320,256]{1,0:T(8,128)(2,1)S(1)}, bf16[320,256]{1,0:T(8,128)(2,1)S(1)}, u32[]{:S(2)}, u32[]{:S(2)}) collective-permute-start(bf16[320,256]{1,0:T(8,128)(2,1)S(1)} %constant_dynamic-update-slice_fusion), channel_id=1, source_target_pairs={{0,1},{1,0},{2,3},{3,2},{4,5},{5,4},{6,7},{7,6},{8,9},{9,8},{10,11... | collective-permute-start | bytes 491528 | tf_op jit(solution)/shard_map/ppermute | solution.py:277
  13.4 5.4 %collective-permute-start.3 = (bf16[320,256]{1,0:T(8,128)(2,1)S(1)}, bf16[320,256]{1,0:T(8,128)(2,1)S(1)}, u32[]{:S(2)}, u32[]{:S(2)}) collective-permute-start(bf16[320,256]{1,0:T(8,128)(2,1)S(1)} %constant_dynamic-update-slice_fusion), channel_id=1, source_target_pairs={{0,4},{1,3},{2,6},{3,1},{4,0},{5,7},{6,2},{7,5},{8,12},{9,11},{10,... | collective-permute-start | bytes 491528 | tf_op jit(solution)/shard_map/ppermute | solution.py:274
  15.6 5.3 %collective-permute-start.2 = (bf16[320,256]{1,0:T(8,128)(2,1)S(1)}, bf16[320,256]{1,0:T(8,128)(2,1)S(1)}, u32[]{:S(2)}, u32[]{:S(2)}) collective-permute-start(bf16[320,256]{1,0:T(8,128)(2,1)S(1)} %collective-permute-done.1.refs_0_), channel_id=1, source_target_pairs={{0,4},{1,3},{2,6},{3,1},{4,0},{5,7},{6,2},{7,5},{8,12},{9,11},{10,... | collective-permute-start | bytes 491528 | tf_op jit(solution)/shard_map/ppermute | solution.py:274
  20.3 4.0 %collective-permute-start.6 = (bf16[320,256]{1,0:T(8,128)(2,1)S(1)}, bf16[320,256]{1,0:T(8,128)(2,1)S(1)}, u32[]{:S(2)}, u32[]{:S(2)}) collective-permute-start(bf16[320,256]{1,0:T(8,128)(2,1)S(1)} %collective-permute-done.1.refs_0_), channel_id=1, source_target_pairs={{0,1},{1,0},{2,3},{3,2},{4,5},{5,4},{6,7},{7,6},{8,9},{9,8},{10,11... | collective-permute-start | bytes 491528 | tf_op jit(solution)/shard_map/ppermute | solution.py:277
  20.6 3.7 %collective-permute-start.7 = (bf16[320,256]{1,0:T(8,128)(2,1)S(1)}, bf16[320,256]{1,0:T(8,128)(2,1)S(1)}, u32[]{:S(2)}, u32[]{:S(2)}) collective-permute-start(bf16[320,256]{1,0:T(8,128)(2,1)S(1)} %collective-permute-done.3.refs_1_), channel_id=1, source_target_pairs={{0,1},{1,0},{2,3},{3,2},{4,5},{5,4},{6,7},{7,6},{8,9},{9,8},{10,11... | collective-permute-start | bytes 491528 | tf_op jit(solution)/shard_map/ppermute | solution.py:277
  20.9 5.3 %collective-permute-start.5 = (bf16[320,256]{1,0:T(8,128)(2,1)S(1)}, bf16[320,256]{1,0:T(8,128)(2,1)S(1)}, u32[]{:S(2)}, u32[]{:S(2)}) collective-permute-start(bf16[320,256]{1,0:T(8,128)(2,1)S(1)} %collective-permute-done.2.refs_0_), channel_id=1, source_target_pairs={{0,1},{1,0},{2,3},{3,2},{4,5},{5,4},{6,7},{7,6},{8,9},{9,8},{10,11... | collective-permute-start | bytes 491528 | tf_op jit(solution)/shard_map/ppermute | solution.py:277

commit v4 on v3

--- a/solution.py
+++ b/solution.py
@@ -11,7 +11,6 @@
 TOPK = 8
 DOCS = 8
 CHUNK = 3584
-FLUSH = 2
 VMEM_LIMIT = 32 * 1024 * 1024
 
 
@@ -54,9 +53,11 @@
     gates = gates_ref[...]
     high = gates.astype(jnp.bfloat16).astype(jnp.float32)
     ids = ids_ref[...].astype(jnp.float32)
-    out_ref[2 * rank : 2 * rank + 16, :] = jnp.concatenate([ids, high], axis=0).astype(jnp.bfloat16)
-    out_ref[2 * rank + 16 :, :] = jnp.concatenate(
-        [gates - high, jnp.zeros_like(gates)], axis=0
+    base = 2 * rank // 16 * tok
+    out_ref[:, base : base + tok] = jnp.concatenate([ids, high], axis=0).astype(jnp.bfloat16)
+    low = gates - high
+    out_ref[:, base + tok :] = jnp.concatenate(
+        [low[:, : tok // 2], low[:, tok // 2 :]], axis=0
     ).astype(jnp.bfloat16)
     start = lax.axis_index("ctx").astype(jnp.int32) * tok
     first = doc_of(offsets_ref, start)
@@ -79,30 +80,40 @@
         copies(i)[2].wait()
         b = b + jnp.dot(g_buf[:, cols], p, preferred_element_type=jnp.float32)[:, rank:]
     both = jnp.concatenate([a, b], axis=1).T
-    out_ref[:rank, :] = both[:rank, :].astype(jnp.bfloat16)
+    for k in range(rank // 16):
+        rows = both[k * 16 : (k + 1) * 16, :]
+        out_ref[:, k * tok : (k + 1) * tok] = rows.astype(jnp.bfloat16)
     scaled = both[rank:, :] * scale
     for j in range(tok // 128):
         lanes = slice(j * 128, (j + 1) * 128)
         rows_buf[j, :, :] = scaled[:, lanes]
         for odd in range(2):
-            picked = rows_buf[j, pl.ds(odd, half, stride=2), :]
-            place = rank + odd * half
-            out_ref[place : place + half, lanes] = picked.astype(jnp.bfloat16)
+            picked = rows_buf[j, pl.ds(odd, half, stride=2), :].astype(jnp.bfloat16)
+            for k in range(half // 16):
+                place = (rank + odd * half + k * 16) // 16 * tok + j * 128
+                out_ref[:, place : place + 128] = picked[k * 16 : (k + 1) * 16, :]
 
 
 def prepare(shape, offsets_ref, ref, base, source):
     rank = shape[1]
     half = rank // 2
-    tok = ref.shape[1]
+    tok = 2 * ref.shape[1] // (4 * rank // 16 + 3)
+
+    def rows(begin, count):
+        parts = [
+            ref[pl.ds(base, 16), k * tok : (k + 1) * tok]
+            for k in range(begin // 16, (begin + count) // 16)
+        ]
+        return jnp.concatenate(parts, axis=0).astype(jnp.float32)
+
     start = source * tok
     first = doc_of(offsets_ref, start)
     position = start + lax.broadcasted_iota(jnp.int32, (1, tok), 1)
     in_first = (position < offsets_ref[first + 1]).astype(jnp.float32)
-    a = ref[pl.ds(base, rank), :].astype(jnp.float32)
-    b = ref[pl.ds(base + rank, rank), :].astype(jnp.float32)
-    named = ref[pl.ds(base + 2 * rank, 16), :].astype(jnp.float32)
-    low = ref[pl.ds(base + 2 * rank + 16, 16), :].astype(jnp.float32)
-    ids, gates = named[:8, :], (named[8:, :] + low[:8, :]) * (EXPERTS / TOPK) ** 0.5
+    a, b, named = rows(0, rank), rows(rank, rank), rows(2 * rank, 16)
+    low = ref[pl.ds(base, 16), (2 * rank // 16 + 1) * tok :].astype(jnp.float32)
+    low = jnp.concatenate([low[:8, :], low[8:, :]], axis=1)
+    ids, gates = named[:8, :], (named[8:, :] + low) * (EXPERTS / TOPK) ** 0.5
     a_first = a * in_first
     a_second = (a - a_first).astype(jnp.bfloat16)
     a_first = a_first.astype(jnp.bfloat16)
@@ -205,23 +216,33 @@
     else:
         ready = []
         add_all(shape, order, blocks, height, offsets_ref, refs, acc, acc)
-    cuts = [experts * k // FLUSH for k in range(FLUSH + 1)]
-    copies = []
-    for k in range(FLUSH):
-        for block in ready:
-            add_block(shape, block, me, acc, acc, cuts[k], cuts[k + 1] + (k == FLUSH - 1))
-        rows = pl.ds(cuts[k] * half, (cuts[k + 1] - cuts[k]) * half)
-        for d in range(DOCS):
-            copies.append(
-                pltpu.make_async_copy(acc.at[d, rows, :], routed_hbm.at[rows, d, :], sem.at[k, d])
-            )
-            copies[-1].start()
+    rows = pl.ds(0, experts * half)
+    copies = [
+        pltpu.make_async_copy(acc.at[d, rows, :], routed_hbm.at[rows, d, :], sem.at[d])
+        for d in range(DOCS)
+    ]
+    touched = [
+        functools.reduce(jnp.logical_or, [doc == d for block in ready for doc in block[0]])
+        if ready
+        else True
+        for d in range(DOCS)
+    ]
+    if ready:
+        for copy, later in zip(copies, touched):
+            pl.when(jnp.logical_not(later))(copy.start)
+    for block in ready:
+        add_block(shape, block, me, acc, acc)
+    for copy, later in zip(copies, touched):
+        if ready:
+            pl.when(later)(copy.start)
+        else:
+            copy.start()
     columns = rank * rank * experts // EXPERTS
     place = experts * half + me * columns // 128
     for j in range(shared_buf.shape[1] // 128):
         for d in range(DOCS):
             shared_buf[d : d + 1, j * 128 : (j + 1) * 128] = acc[d, pl.ds(place + j, 1), :]
-    copies.append(pltpu.make_async_copy(shared_buf, shared_hbm, sem.at[FLUSH, 0]))
+    copies.append(pltpu.make_async_copy(shared_buf, shared_hbm, sem.at[DOCS]))
     copies[-1].start()
     for copy in copies:
         copy.wait()
@@ -232,7 +253,7 @@
     rank = projections.shape[1] // 2
     half = rank // 2
     experts = EXPERTS // devices
-    height = 2 * rank + 32
+    height, width = 16, tok * (2 * rank // 16) + tok + tok // 2
     smem = pl.BlockSpec(memory_space=pltpu.SMEM)
     vmem = pl.BlockSpec(memory_space=pltpu.VMEM)
     hbm = pl.BlockSpec(memory_space=pltpu.HBM)
@@ -245,7 +266,7 @@
     payload, offsets = pl.pallas_call(
         project_kernel,
         out_shape=(
-            pltpu.VMEM((height, tok), jnp.bfloat16),
+            pltpu.VMEM((height, width), jnp.bfloat16),
             pltpu.SMEM(offsets.shape, jnp.int32),
         ),
         in_specs=[hbm] * 6,
@@ -312,13 +333,14 @@
     near_core = core(near)
     one, acc = after(one, acc)
     three = swap(one, last)
-    acc = add("sums_next", [(one, bits[0], 0), (two, bits[1], 0), (near_core, 0, 1)], acc)
-    one, two, acc = lax.optimization_barrier((one, two, acc))
-    one_core, two_core = core(one), core(two)
+    one_core = core(one)
+    blocks = [(one, bits[0], 0), (two, bits[1], 0), (near_core, 0, 1), (one_core, bits[0], 1)]
+    acc = add("sums_next", blocks, acc)
+    two, acc = after(two, acc)
+    two_core = core(two)
     three, acc = after(three, acc)
     three_core = core(three)
-    blocks = [(three, both, 0), (one_core, bits[0], 1), (two_core, bits[1], 1)]
-    acc = add("sums_three", blocks, acc, fold=True)
+    acc = add("sums_three", [(three, both, 0), (two_core, bits[1], 1)], acc, fold=True)
     three_core, acc = after(three_core, acc)
     blocks = [(three_core, both, 1)]
     columns = rank * rank // devices
@@ -333,7 +355,7 @@
         out_specs=(hbm, hbm, vmem),
         scratch_shapes=[
             pltpu.VMEM((DOCS, max(columns, 128)), jnp.float32),
-            pltpu.SemaphoreType.DMA((FLUSH + 1, DOCS)),
+            pltpu.SemaphoreType.DMA((DOCS + 1,)),
         ],
         input_output_aliases={1: 2},
         compiler_params=params,

time: 28.4 us -> 27.3 us (0.961)
  the two profiles are of different devices: /device:TPU:27 before, /device:TPU:0 now
where the time goes in v4:
time: 27.3 us; the launch traced here: 26.9 us
  Pallas kernels  10.9 us (40%)
  starting transfers between devices  10.4 us (38%)
  waiting for transfers between devices  4.91 us (18%)
  between operations  0.69 us (3%)
    ppermute x4, starting transfers between devices, swap(): lax.ppermute(block, 'ctx', [(i, i ^ order[i & 1][k]) for i in range(devic...  9.01 us
    pallas_call x1, Pallas kernels, on_device(): pl.pallas_call(project_kernel, out_shape=(pltpu.VMEM((height, width), jnp...  4.89 us
    ppermute x4, waiting for transfers between devices, swap(): lax.ppermute(block, 'ctx', [(i, i ^ order[i & 1][k]) for i in range(devic...  4.45 us
    pallas_call x4, Pallas kernels, add(): pl.pallas_call(functools.partial(kernel, shape, order, [b[1:] for b in bl...  4.36 us
    pallas_call x1, Pallas kernels, on_device(): pl.pallas_call(functools.partial(last_kernel, shape, order, [b[1:] for b...  1.63 us
    ppermute x4, starting transfers between devices, core(): return lax.ppermute(block, 'ctx', [(i, i ^ 1) for i in range(devices)])  1.39 us
  transfers between devices with their start and end apart: 8, of which 5 were waited for; matrix products, arithmetic and copies ran while one was open for 0% of the time, Pallas kernels for 16%

profile of v4, /device:TPU:0, one launch (start us, length us, event | category | flops | bytes accessed | tf_op | source)
XLA Modules:
  0.0 26.9 jit_solution(10139946746717981433)
XLA Ops:
  0.6 4.9 %project.1 = (bf16[16,2432]{1,0:T(8,128)(2,1)S(1)}, s32[9]{0:T(128)S(4)}) custom-call(f32[8,256]{1,0:T(8,128)} %bitcast.7, s32[8,256]{1,0:T(8,128)} %bitcast.8, s32[9]{0:T(128)} %offsets_hbm.1, bf16[256,7168]{1,0:T(8,128)(2,1)} %x_hbm.1, bf16[256,7168]{1,0:T(8,128)(2,1)} %g_hbm.1, bf16[7168,128]{1,0:T(8,128)(2,1)} %p_hbm.1), custom_call_target="tpu_custom_call" | custom-call | tf_op jit(solution)/shard_map/project/pallas_call | solution.py:266
  5.5 4.1 %collective-permute-start = (bf16[16,2432]{1,0:T(8,128)(2,1)S(1)}, bf16[16,2432]{1,0:T(8,128)(2,1)S(1)}, u32[]{:S(2)}, u32[]{:S(2)}) collective-permute-start(bf16[16,2432]{1,0:T(8,128)(2,1)S(1)} %get-tuple-element.30.refs_0_), channel_id=1, source_target_pairs={{0,8},{1,5},{2,10},{3,7},{4,12},{5,1},{6,14},{7,3},{8,0},{9,13},{1... | collective-permute-start | bytes 233480 | tf_op jit(solution)/shard_map/ppermute | solution.py:295
  9.6 0.6 %sums_own.1 = (f32[8,544,128]{2,1,0:T(8,128)S(1)}, f32[8,544,128]{2,1,0:T(8,128)S(1)}) custom-call(s32[9]{0:T(128)S(4)} %get-tuple-element.29.offsets_ref, bf16[16,2432]{1,0:T(8,128)(2,1)S(1)} %get-tuple-element.30.refs_0_), custom_call_target="tpu_custom_call" | custom-call | tf_op jit(solution)/shard_map/sums_own/pallas_call | solution.py:309
  10.3 1.7 %collective-permute-done.refs_0_ = bf16[16,2432]{1,0:T(8,128)(2,1)S(1)} collective-permute-done((bf16[16,2432]{1,0:T(8,128)(2,1)S(1)}, bf16[16,2432]{1,0:T(8,128)(2,1)S(1)}, u32[]{:S(2)}, u32[]{:S(2)}) %collective-permute-start) | collective-permute-done | bytes 77856 | tf_op jit(solution)/shard_map/ppermute | solution.py:295
  12.0 1.9 %collective-permute-start.1 = (bf16[32,2432]{1,0:T(8,128)(2,1)S(1)}, bf16[32,2432]{1,0:T(8,128)(2,1)S(1)}, u32[]{:S(2)}, u32[]{:S(2)}) collective-permute-start(bf16[32,2432]{1,0:T(8,128)(2,1)S(1)} %constant_dynamic-update-slice_fusion), channel_id=1, source_target_pairs={{0,2},{1,9},{2,0},{3,11},{4,6},{5,13},{6,4},{7,15},{8,10},{9,1},{1... | collective-permute-start | bytes 466952 | tf_op jit(solution)/shard_map/ppermute | solution.py:295
  13.9 0.4 %sums_got.1 = (f32[8,544,128]{2,1,0:T(8,128)S(1)}, f32[8,544,128]{2,1,0:T(8,128)S(1)}) custom-call(s32[9]{0:T(128)S(4)} %get-tuple-element.29.offsets_ref, f32[8,544,128]{2,1,0:T(8,128)S(1)} %get-tuple-element.34.acc_in, f32[8,544,128]{2,1,0:T(8,128)S(1)} %get-tuple-element.35.again_in, ...), custom_call_target="tpu_custom_call", output_to_operand_aliasing={{0}: (1, {}), {1}: (2, {})} | custom-call | tf_op jit(solution)/shard_map/sums_got/pallas_call | solution.py:309
  14.3 0.1 collective-permute-start.4
  14.4 1.6 %collective-permute-start.3 = (bf16[32,2432]{1,0:T(8,128)(2,1)S(1)}, bf16[32,2432]{1,0:T(8,128)(2,1)S(1)}, u32[]{:S(2)}, u32[]{:S(2)}) collective-permute-start(bf16[32,2432]{1,0:T(8,128)(2,1)S(1)} %constant_dynamic-update-slice_fusion), channel_id=1, source_target_pairs={{0,4},{1,3},{2,6},{3,1},{4,0},{5,7},{6,2},{7,5},{8,12},{9,11},{10,... | collective-permute-start | bytes 466952 | tf_op jit(solution)/shard_map/ppermute | solution.py:295
  16.0 2.1 %collective-permute-done.1.refs_0_ = bf16[32,2432]{1,0:T(8,128)(2,1)S(1)} collective-permute-done((bf16[32,2432]{1,0:T(8,128)(2,1)S(1)}, bf16[32,2432]{1,0:T(8,128)(2,1)S(1)}, u32[]{:S(2)}, u32[]{:S(2)}) %collective-permute-start.1) | collective-permute-done | bytes 155680 | tf_op jit(solution)/shard_map/ppermute | solution.py:295
  18.1 0.0 collective-permute-start.5
  18.1 1.4 %collective-permute-start.2 = (bf16[32,2432]{1,0:T(8,128)(2,1)S(1)}, bf16[32,2432]{1,0:T(8,128)(2,1)S(1)}, u32[]{:S(2)}, u32[]{:S(2)}) collective-permute-start(bf16[32,2432]{1,0:T(8,128)(2,1)S(1)} %collective-permute-done.1.refs_0_), channel_id=1, source_target_pairs={{0,4},{1,3},{2,6},{3,1},{4,0},{5,7},{6,2},{7,5},{8,12},{9,11},{10,... | collective-permute-start | bytes 466952 | tf_op jit(solution)/shard_map/ppermute | solution.py:295
  19.5 0.0 collective-permute-done.4.refs_2_
  19.5 0.2 collective-permute-done.3.refs_1_
  19.7 0.0 collective-permute-done.5.refs_3_
  19.7 2.0 %sums_next.1 = (f32[8,544,128]{2,1,0:T(8,128)S(1)}, f32[8,544,128]{2,1,0:T(8,128)S(1)}) custom-call(s32[9]{0:T(128)S(4)} %get-tuple-element.29.offsets_ref, f32[8,544,128]{2,1,0:T(8,128)S(1)} %get-tuple-element.42.acc_in, f32[8,544,128]{2,1,0:T(8,128)S(1)} %get-tuple-element.43.again_in, ...), custom_call_target="tpu_custom_call", output_to_operand_aliasing={{0}: (1, {}), {1}: (2, {})} | custom-call | tf_op jit(solution)/shard_map/sums_next/pallas_call | solution.py:309
  21.7 1.2 %collective-permute-start.7 = (bf16[32,2432]{1,0:T(8,128)(2,1)S(1)}, bf16[32,2432]{1,0:T(8,128)(2,1)S(1)}, u32[]{:S(2)}, u32[]{:S(2)}) collective-permute-start(bf16[32,2432]{1,0:T(8,128)(2,1)S(1)} %collective-permute-done.3.refs_1_), channel_id=1, source_target_pairs={{0,1},{1,0},{2,3},{3,2},{4,5},{5,4},{6,7},{7,6},{8,9},{9,8},{10,11... | collective-permute-start | bytes 466952 | tf_op jit(solution)/shard_map/ppermute | solution.py:298
  22.9 0.4 %collective-permute-done.2.refs_0_ = bf16[32,2432]{1,0:T(8,128)(2,1)S(1)} collective-permute-done((bf16[32,2432]{1,0:T(8,128)(2,1)S(1)}, bf16[32,2432]{1,0:T(8,128)(2,1)S(1)}, u32[]{:S(2)}, u32[]{:S(2)}) %collective-permute-start.2) | collective-permute-done | bytes 155680 | tf_op jit(solution)/shard_map/ppermute | solution.py:295
  23.3 0.1 collective-permute-start.6
  23.4 0.5 %collective-permute-done.7.refs_1_ = bf16[32,2432]{1,0:T(8,128)(2,1)S(1)} collective-permute-done((bf16[32,2432]{1,0:T(8,128)(2,1)S(1)}, bf16[32,2432]{1,0:T(8,128)(2,1)S(1)}, u32[]{:S(2)}, u32[]{:S(2)}) %collective-permute-start.7) | collective-permute-done | bytes 155680 | tf_op jit(solution)/shard_map/ppermute | solution.py:298
  23.9 1.4 %sums_three.1.held = f32[8,544,128]{2,1,0:T(8,128)S(1)} custom-call(s32[9]{0:T(128)S(4)} %get-tuple-element.29.offsets_ref, f32[8,544,128]{2,1,0:T(8,128)S(1)} %get-tuple-element.49.acc_in, f32[8,544,128]{2,1,0:T(8,128)S(1)} %get-tuple-element.50.again, bf16[32,2432]{1,0:T(8,128)(2,1)S(1)} %collective-permute-done.2.refs_0_, ...), custom_call_target="tpu_custom_call", output_to_operand_aliasing={{}: (1, {})} | custom-call | tf_op jit(solution)/shard_map/sums_three/pallas_call | solution.py:309
  25.3 0.0 collective-permute-done.6.refs_0_
  25.3 1.6 %sums_last.1 = (f32[512,8,128]{2,1,0:T(8,128)}, f32[8,256]{1,0:T(8,128)}, f32[8,544,128]{2,1,0:T(8,128)S(1)}) custom-call(s32[9]{0:T(128)S(4)} %get-tuple-element.29.offsets_ref, f32[8,544,128]{2,1,0:T(8,128)S(1)} %sums_three.1.held, bf16[32,2432]{1,0:T(8,128)(2,1)S(1)} %collective-permute-done.6.refs_0_), custom_call_target="tpu_custom_call", output_to_operand_aliasing={{2}: (1, {})} | custom-call | tf_op jit(solution)/shard_map/sums_last/pallas_call | solution.py:347
  (2 shorter events, 0.0 us)
Async XLA Ops:
  5.5 6.5 %collective-permute-start = (bf16[16,2432]{1,0:T(8,128)(2,1)S(1)}, bf16[16,2432]{1,0:T(8,128)(2,1)S(1)}, u32[]{:S(2)}, u32[]{:S(2)}) collective-permute-start(bf16[16,2432]{1,0:T(8,128)(2,1)S(1)} %get-tuple-element.30.refs_0_), channel_id=1, source_target_pairs={{0,8},{1,5},{2,10},{3,7},{4,12},{5,1},{6,14},{7,3},{8,0},{9,13},{1... | collective-permute-start | bytes 233480 | tf_op jit(solution)/shard_map/ppermute | solution.py:295
  12.0 6.0 %collective-permute-start.1 = (bf16[32,2432]{1,0:T(8,128)(2,1)S(1)}, bf16[32,2432]{1,0:T(8,128)(2,1)S(1)}, u32[]{:S(2)}, u32[]{:S(2)}) collective-permute-start(bf16[32,2432]{1,0:T(8,128)(2,1)S(1)} %constant_dynamic-update-slice_fusion), channel_id=1, source_target_pairs={{0,2},{1,9},{2,0},{3,11},{4,6},{5,13},{6,4},{7,15},{8,10},{9,1},{1... | collective-permute-start | bytes 466952 | tf_op jit(solution)/shard_map/ppermute | solution.py:295
  14.3 5.2 %collective-permute-start.4 = (bf16[32,2432]{1,0:T(8,128)(2,1)S(1)}, bf16[32,2432]{1,0:T(8,128)(2,1)S(1)}, u32[]{:S(2)}, u32[]{:S(2)}) collective-permute-start(bf16[32,2432]{1,0:T(8,128)(2,1)S(1)} %constant_dynamic-update-slice_fusion), channel_id=1, source_target_pairs={{0,1},{1,0},{2,3},{3,2},{4,5},{5,4},{6,7},{7,6},{8,9},{9,8},{10,11... | collective-permute-start | bytes 466952 | tf_op jit(solution)/shard_map/ppermute | solution.py:298
  14.4 5.3 %collective-permute-start.3 = (bf16[32,2432]{1,0:T(8,128)(2,1)S(1)}, bf16[32,2432]{1,0:T(8,128)(2,1)S(1)}, u32[]{:S(2)}, u32[]{:S(2)}) collective-permute-start(bf16[32,2432]{1,0:T(8,128)(2,1)S(1)} %constant_dynamic-update-slice_fusion), channel_id=1, source_target_pairs={{0,4},{1,3},{2,6},{3,1},{4,0},{5,7},{6,2},{7,5},{8,12},{9,11},{10,... | collective-permute-start | bytes 466952 | tf_op jit(solution)/shard_map/ppermute | solution.py:295
  18.1 1.6 %collective-permute-start.5 = (bf16[32,2432]{1,0:T(8,128)(2,1)S(1)}, bf16[32,2432]{1,0:T(8,128)(2,1)S(1)}, u32[]{:S(2)}, u32[]{:S(2)}) collective-permute-start(bf16[32,2432]{1,0:T(8,128)(2,1)S(1)} %collective-permute-done.1.refs_0_), channel_id=1, source_target_pairs={{0,1},{1,0},{2,3},{3,2},{4,5},{5,4},{6,7},{7,6},{8,9},{9,8},{10,11... | collective-permute-start | bytes 466952 | tf_op jit(solution)/shard_map/ppermute | solution.py:298
  18.1 5.2 %collective-permute-start.2 = (bf16[32,2432]{1,0:T(8,128)(2,1)S(1)}, bf16[32,2432]{1,0:T(8,128)(2,1)S(1)}, u32[]{:S(2)}, u32[]{:S(2)}) collective-permute-start(bf16[32,2432]{1,0:T(8,128)(2,1)S(1)} %collective-permute-done.1.refs_0_), channel_id=1, source_target_pairs={{0,4},{1,3},{2,6},{3,1},{4,0},{5,7},{6,2},{7,5},{8,12},{9,11},{10,... | collective-permute-start | bytes 466952 | tf_op jit(solution)/shard_map/ppermute | solution.py:295
  21.7 2.2 %collective-permute-start.7 = (bf16[32,2432]{1,0:T(8,128)(2,1)S(1)}, bf16[32,2432]{1,0:T(8,128)(2,1)S(1)}, u32[]{:S(2)}, u32[]{:S(2)}) collective-permute-start(bf16[32,2432]{1,0:T(8,128)(2,1)S(1)} %collective-permute-done.3.refs_1_), channel_id=1, source_target_pairs={{0,1},{1,0},{2,3},{3,2},{4,5},{5,4},{6,7},{7,6},{8,9},{9,8},{10,11... | collective-permute-start | bytes 466952 | tf_op jit(solution)/shard_map/ppermute | solution.py:298
  23.3 2.0 %collective-permute-start.6 = (bf16[32,2432]{1,0:T(8,128)(2,1)S(1)}, bf16[32,2432]{1,0:T(8,128)(2,1)S(1)}, u32[]{:S(2)}, u32[]{:S(2)}) collective-permute-start(bf16[32,2432]{1,0:T(8,128)(2,1)S(1)} %collective-permute-done.2.refs_0_), channel_id=1, source_target_pairs={{0,1},{1,0},{2,3},{3,2},{4,5},{5,4},{6,7},{7,6},{8,9},{9,8},{10,11... | collective-permute-start | bytes 466952 | tf_op jit(solution)/shard_map/ppermute | solution.py:298

commit v5 on v4

--- a/solution.py
+++ b/solution.py
@@ -320,6 +320,9 @@
     acc = add("sums_own", [(payload, 0, 0)])
     for k in range(last - 1):
         got = swap(near, k)
+        if k == last - 2:
+            early, acc = after(near, acc)
+            two_early = swap(early, last)
         got, acc = after(got, acc)
         near = jnp.concatenate([near, got], axis=0)
         if k < last - 2:
@@ -328,8 +331,8 @@
     both = bits[0] | bits[1]
     one = swap(near, last - 1)
     acc = add("sums_got", [(got, 1 << (last - 2), 0)], acc)
-    near, acc = after(near, acc)
-    two = swap(near, last)
+    near, late, acc = lax.optimization_barrier((near, got, acc))
+    two = jnp.concatenate([two_early, swap(late, last)], axis=0)
     near_core = core(near)
     one, acc = after(one, acc)
     three = swap(one, last)

time: 27.3 us -> 26.6 us (0.974)
  waiting for transfers between devices: 4.91 us -> 3.62 us
  starting transfers between devices: 10.4 us -> 11.1 us
    ppermute x4 -> x5, starting transfers between devices: 9.01 us -> 10.8 us  [swap(): lax.ppermute(block, 'ctx', [(i, i ^ order[i & 1][k]) for i in range(devic...]
    ppermute x4, starting transfers between devices: 1.39 us -> 0.22 us  [core(): return lax.ppermute(block, 'ctx', [(i, i ^ 1) for i in range(devices)])]
    ppermute x4 -> x5, waiting for transfers between devices: 4.45 us -> 3.61 us  [swap(): lax.ppermute(block, 'ctx', [(i, i ^ order[i & 1][k]) for i in range(devic...]
    ppermute x4, waiting for transfers between devices: 0.46 us -> 0.01 us  [core(): return lax.ppermute(block, 'ctx', [(i, i ^ 1) for i in range(devices)])]
  transfers between devices with their start and end apart: 8 -> 9, of which waited for: 5 -> 3; matrix products, arithmetic and copies ran while one was open for 0% -> 0% of each run, Pallas kernels for 16% -> 17%
where the time goes in v5:
time: 26.6 us; the launch traced here: 26.3 us
  starting transfers between devices  11.1 us (42%)
  Pallas kernels  10.9 us (41%)
  waiting for transfers between devices  3.62 us (14%)
  between operations  0.71 us (3%)
    ppermute x5, starting transfers between devices, swap(): lax.ppermute(block, 'ctx', [(i, i ^ order[i & 1][k]) for i in range(devic...  10.8 us
    pallas_call x1, Pallas kernels, on_device(): pl.pallas_call(project_kernel, out_shape=(pltpu.VMEM((height, width), jnp...  4.89 us
    pallas_call x4, Pallas kernels, add(): pl.pallas_call(functools.partial(kernel, shape, order, [b[1:] for b in bl...  4.37 us
    ppermute x5, waiting for transfers between devices, swap(): lax.ppermute(block, 'ctx', [(i, i ^ order[i & 1][k]) for i in range(devic...  3.61 us
    pallas_call x1, Pallas kernels, on_device(): pl.pallas_call(functools.partial(last_kernel, shape, order, [b[1:] for b...  1.64 us
  transfers between devices with their start and end apart: 9, of which 3 were waited for; matrix products, arithmetic and copies ran while one was open for 0% of the time, Pallas kernels for 17%

profile of v5, /device:TPU:0, one launch (start us, length us, event | category | flops | bytes accessed | tf_op | source)
XLA Modules:
  0.0 26.3 jit_solution(17592761484415816685)
XLA Ops:
  0.6 4.9 %project.1 = (bf16[16,2432]{1,0:T(8,128)(2,1)S(1)}, s32[9]{0:T(128)S(4)}) custom-call(f32[8,256]{1,0:T(8,128)} %bitcast.7, s32[8,256]{1,0:T(8,128)} %bitcast.8, s32[9]{0:T(128)} %offsets_hbm.1, bf16[256,7168]{1,0:T(8,128)(2,1)} %x_hbm.1, bf16[256,7168]{1,0:T(8,128)(2,1)} %g_hbm.1, bf16[7168,128]{1,0:T(8,128)(2,1)} %p_hbm.1), custom_call_target="tpu_custom_call" | custom-call | tf_op jit(solution)/shard_map/project/pallas_call | solution.py:266
  5.5 4.1 %collective-permute-start = (bf16[16,2432]{1,0:T(8,128)(2,1)S(1)}, bf16[16,2432]{1,0:T(8,128)(2,1)S(1)}, u32[]{:S(2)}, u32[]{:S(2)}) collective-permute-start(bf16[16,2432]{1,0:T(8,128)(2,1)S(1)} %get-tuple-element.47.refs_0_), channel_id=1, source_target_pairs={{0,8},{1,5},{2,10},{3,7},{4,12},{5,1},{6,14},{7,3},{8,0},{9,13},{1... | collective-permute-start | bytes 233480 | tf_op jit(solution)/shard_map/ppermute | solution.py:295
  9.6 0.6 %sums_own.1 = (f32[8,544,128]{2,1,0:T(8,128)S(1)}, f32[8,544,128]{2,1,0:T(8,128)S(1)}) custom-call(s32[9]{0:T(128)S(4)} %get-tuple-element.33.offsets_ref, bf16[16,2432]{1,0:T(8,128)(2,1)S(1)} %get-tuple-element.47.refs_0_), custom_call_target="tpu_custom_call" | custom-call | tf_op jit(solution)/shard_map/sums_own/pallas_call | solution.py:309
  10.3 1.6 %collective-permute-start.3 = (bf16[16,2432]{1,0:T(8,128)(2,1)S(1)}, bf16[16,2432]{1,0:T(8,128)(2,1)S(1)}, u32[]{:S(2)}, u32[]{:S(2)}) collective-permute-start(bf16[16,2432]{1,0:T(8,128)(2,1)S(1)} %get-tuple-element.47.refs_0_), channel_id=1, source_target_pairs={{0,4},{1,3},{2,6},{3,1},{4,0},{5,7},{6,2},{7,5},{8,12},{9,11},{10,... | collective-permute-start | bytes 233480 | tf_op jit(solution)/shard_map/ppermute | solution.py:295
  11.9 0.1 collective-permute-done.refs_0_
  12.0 1.9 %collective-permute-start.1 = (bf16[32,2432]{1,0:T(8,128)(2,1)S(1)}, bf16[32,2432]{1,0:T(8,128)(2,1)S(1)}, u32[]{:S(2)}, u32[]{:S(2)}) collective-permute-start(bf16[32,2432]{1,0:T(8,128)(2,1)S(1)} %constant_dynamic-update-slice_fusion), channel_id=1, source_target_pairs={{0,2},{1,9},{2,0},{3,11},{4,6},{5,13},{6,4},{7,15},{8,10},{9,1},{1... | collective-permute-start | bytes 466952 | tf_op jit(solution)/shard_map/ppermute | solution.py:295
  13.9 0.4 %sums_got.1 = (f32[8,544,128]{2,1,0:T(8,128)S(1)}, f32[8,544,128]{2,1,0:T(8,128)S(1)}) custom-call(s32[9]{0:T(128)S(4)} %get-tuple-element.33.offsets_ref, f32[8,544,128]{2,1,0:T(8,128)S(1)} %get-tuple-element.40.acc_in, f32[8,544,128]{2,1,0:T(8,128)S(1)} %get-tuple-element.41.again_in, ...), custom_call_target="tpu_custom_call", output_to_operand_aliasing={{0}: (1, {}), {1}: (2, {})} | custom-call | tf_op jit(solution)/shard_map/sums_got/pallas_call | solution.py:309
  14.3 1.6 %collective-permute-start.4 = (bf16[16,2432]{1,0:T(8,128)(2,1)S(1)}, bf16[16,2432]{1,0:T(8,128)(2,1)S(1)}, u32[]{:S(2)}, u32[]{:S(2)}) collective-permute-start(bf16[16,2432]{1,0:T(8,128)(2,1)S(1)} %collective-permute-done.refs_0_), channel_id=1, source_target_pairs={{0,4},{1,3},{2,6},{3,1},{4,0},{5,7},{6,2},{7,5},{8,12},{9,11},{10,... | collective-permute-start | bytes 233480 | tf_op jit(solution)/shard_map/ppermute | solution.py:295
  15.9 0.0 collective-permute-start.5
  15.9 0.0 collective-permute-done.3
  15.9 2.1 %collective-permute-done.1.refs_0_ = bf16[32,2432]{1,0:T(8,128)(2,1)S(1)} collective-permute-done((bf16[32,2432]{1,0:T(8,128)(2,1)S(1)}, bf16[32,2432]{1,0:T(8,128)(2,1)S(1)}, u32[]{:S(2)}, u32[]{:S(2)}) %collective-permute-start.1) | collective-permute-done | bytes 155680 | tf_op jit(solution)/shard_map/ppermute | solution.py:295
  18.0 0.0 collective-permute-start.6
  18.0 1.6 %collective-permute-start.2 = (bf16[32,2432]{1,0:T(8,128)(2,1)S(1)}, bf16[32,2432]{1,0:T(8,128)(2,1)S(1)}, u32[]{:S(2)}, u32[]{:S(2)}) collective-permute-start(bf16[32,2432]{1,0:T(8,128)(2,1)S(1)} %collective-permute-done.1.refs_0_), channel_id=1, source_target_pairs={{0,4},{1,3},{2,6},{3,1},{4,0},{5,7},{6,2},{7,5},{8,12},{9,11},{10,... | collective-permute-start | bytes 466952 | tf_op jit(solution)/shard_map/ppermute | solution.py:295
  19.6 0.0 collective-permute-done.4
  19.6 0.0 collective-permute-done.5.refs_2_
  19.6 0.0 collective-permute-done.6.refs_3_
  19.7 2.0 %sums_next.1 = (f32[8,544,128]{2,1,0:T(8,128)S(1)}, f32[8,544,128]{2,1,0:T(8,128)S(1)}) custom-call(s32[9]{0:T(128)S(4)} %get-tuple-element.33.offsets_ref, f32[8,544,128]{2,1,0:T(8,128)S(1)} %get-tuple-element.49.acc_in, f32[8,544,128]{2,1,0:T(8,128)S(1)} %get-tuple-element.50.again_in, ...), custom_call_target="tpu_custom_call", output_to_operand_aliasing={{0}: (1, {}), {1}: (2, {})} | custom-call | tf_op jit(solution)/shard_map/sums_next/pallas_call | solution.py:309
  21.7 0.2 collective-permute-start.8
  21.9 1.4 %collective-permute-done.2.refs_0_ = bf16[32,2432]{1,0:T(8,128)(2,1)S(1)} collective-permute-done((bf16[32,2432]{1,0:T(8,128)(2,1)S(1)}, bf16[32,2432]{1,0:T(8,128)(2,1)S(1)}, u32[]{:S(2)}, u32[]{:S(2)}) %collective-permute-start.2) | collective-permute-done | bytes 155680 | tf_op jit(solution)/shard_map/ppermute | solution.py:295
  23.3 0.0 collective-permute-start.7
  23.3 0.0 collective-permute-done.8.refs_1_
  23.3 1.4 %sums_three.1.held = f32[8,544,128]{2,1,0:T(8,128)S(1)} custom-call(s32[9]{0:T(128)S(4)} %get-tuple-element.33.offsets_ref, f32[8,544,128]{2,1,0:T(8,128)S(1)} %get-tuple-element.57.acc_in, f32[8,544,128]{2,1,0:T(8,128)S(1)} %get-tuple-element.58.again, bf16[32,2432]{1,0:T(8,128)(2,1)S(1)} %collective-permute-done.2.refs_0_, ...), custom_call_target="tpu_custom_call", output_to_operand_aliasing={{}: (1, {})} | custom-call | tf_op jit(solution)/shard_map/sums_three/pallas_call | solution.py:309
  24.7 0.0 collective-permute-done.7.refs_0_
  24.7 1.6 %sums_last.1 = (f32[512,8,128]{2,1,0:T(8,128)}, f32[8,256]{1,0:T(8,128)}, f32[8,544,128]{2,1,0:T(8,128)S(1)}) custom-call(s32[9]{0:T(128)S(4)} %get-tuple-element.33.offsets_ref, f32[8,544,128]{2,1,0:T(8,128)S(1)} %sums_three.1.held, bf16[32,2432]{1,0:T(8,128)(2,1)S(1)} %collective-permute-done.7.refs_0_), custom_call_target="tpu_custom_call", output_to_operand_aliasing={{2}: (1, {})} | custom-call | tf_op jit(solution)/shard_map/sums_last/pallas_call | solution.py:350
  (4 shorter events, 0.0 us)
Async XLA Ops:
  5.5 6.5 %collective-permute-start = (bf16[16,2432]{1,0:T(8,128)(2,1)S(1)}, bf16[16,2432]{1,0:T(8,128)(2,1)S(1)}, u32[]{:S(2)}, u32[]{:S(2)}) collective-permute-start(bf16[16,2432]{1,0:T(8,128)(2,1)S(1)} %get-tuple-element.47.refs_0_), channel_id=1, source_target_pairs={{0,8},{1,5},{2,10},{3,7},{4,12},{5,1},{6,14},{7,3},{8,0},{9,13},{1... | collective-permute-start | bytes 233480 | tf_op jit(solution)/shard_map/ppermute | solution.py:295
  10.3 5.7 %collective-permute-start.3 = (bf16[16,2432]{1,0:T(8,128)(2,1)S(1)}, bf16[16,2432]{1,0:T(8,128)(2,1)S(1)}, u32[]{:S(2)}, u32[]{:S(2)}) collective-permute-start(bf16[16,2432]{1,0:T(8,128)(2,1)S(1)} %get-tuple-element.47.refs_0_), channel_id=1, source_target_pairs={{0,4},{1,3},{2,6},{3,1},{4,0},{5,7},{6,2},{7,5},{8,12},{9,11},{10,... | collective-permute-start | bytes 233480 | tf_op jit(solution)/shard_map/ppermute | solution.py:295
  12.0 6.0 %collective-permute-start.1 = (bf16[32,2432]{1,0:T(8,128)(2,1)S(1)}, bf16[32,2432]{1,0:T(8,128)(2,1)S(1)}, u32[]{:S(2)}, u32[]{:S(2)}) collective-permute-start(bf16[32,2432]{1,0:T(8,128)(2,1)S(1)} %constant_dynamic-update-slice_fusion), channel_id=1, source_target_pairs={{0,2},{1,9},{2,0},{3,11},{4,6},{5,13},{6,4},{7,15},{8,10},{9,1},{1... | collective-permute-start | bytes 466952 | tf_op jit(solution)/shard_map/ppermute | solution.py:295
  14.3 5.3 %collective-permute-start.4 = (bf16[16,2432]{1,0:T(8,128)(2,1)S(1)}, bf16[16,2432]{1,0:T(8,128)(2,1)S(1)}, u32[]{:S(2)}, u32[]{:S(2)}) collective-permute-start(bf16[16,2432]{1,0:T(8,128)(2,1)S(1)} %collective-permute-done.refs_0_), channel_id=1, source_target_pairs={{0,4},{1,3},{2,6},{3,1},{4,0},{5,7},{6,2},{7,5},{8,12},{9,11},{10,... | collective-permute-start | bytes 233480 | tf_op jit(solution)/shard_map/ppermute | solution.py:295
  15.9 3.7 %collective-permute-start.5 = (bf16[32,2432]{1,0:T(8,128)(2,1)S(1)}, bf16[32,2432]{1,0:T(8,128)(2,1)S(1)}, u32[]{:S(2)}, u32[]{:S(2)}) collective-permute-start(bf16[32,2432]{1,0:T(8,128)(2,1)S(1)} %constant_dynamic-update-slice_fusion), channel_id=1, source_target_pairs={{0,1},{1,0},{2,3},{3,2},{4,5},{5,4},{6,7},{7,6},{8,9},{9,8},{10,11... | collective-permute-start | bytes 466952 | tf_op jit(solution)/shard_map/ppermute | solution.py:298
  18.0 1.6 %collective-permute-start.6 = (bf16[32,2432]{1,0:T(8,128)(2,1)S(1)}, bf16[32,2432]{1,0:T(8,128)(2,1)S(1)}, u32[]{:S(2)}, u32[]{:S(2)}) collective-permute-start(bf16[32,2432]{1,0:T(8,128)(2,1)S(1)} %collective-permute-done.1.refs_0_), channel_id=1, source_target_pairs={{0,1},{1,0},{2,3},{3,2},{4,5},{5,4},{6,7},{7,6},{8,9},{9,8},{10,11... | collective-permute-start | bytes 466952 | tf_op jit(solution)/shard_map/ppermute | solution.py:298
  18.0 5.2 %collective-permute-start.2 = (bf16[32,2432]{1,0:T(8,128)(2,1)S(1)}, bf16[32,2432]{1,0:T(8,128)(2,1)S(1)}, u32[]{:S(2)}, u32[]{:S(2)}) collective-permute-start(bf16[32,2432]{1,0:T(8,128)(2,1)S(1)} %collective-permute-done.1.refs_0_), channel_id=1, source_target_pairs={{0,4},{1,3},{2,6},{3,1},{4,0},{5,7},{6,2},{7,5},{8,12},{9,11},{10,... | collective-permute-start | bytes 466952 | tf_op jit(solution)/shard_map/ppermute | solution.py:295
  21.7 1.6 %collective-permute-start.8 = (bf16[32,2432]{1,0:T(8,128)(2,1)S(1)}, bf16[32,2432]{1,0:T(8,128)(2,1)S(1)}, u32[]{:S(2)}, u32[]{:S(2)}) collective-permute-start(bf16[32,2432]{1,0:T(8,128)(2,1)S(1)} %constant_dynamic-update-slice_fusion.2.refs_1_), channel_id=1, source_target_pairs={{0,1},{1,0},{2,3},{3,2},{4,5},{5,4},{6,7},{7,6},{8,9},{9,8},{10,11... | collective-permute-start | bytes 466952 | tf_op jit(solution)/shard_map/ppermute | solution.py:298
  23.3 1.4 %collective-permute-start.7 = (bf16[32,2432]{1,0:T(8,128)(2,1)S(1)}, bf16[32,2432]{1,0:T(8,128)(2,1)S(1)}, u32[]{:S(2)}, u32[]{:S(2)}) collective-permute-start(bf16[32,2432]{1,0:T(8,128)(2,1)S(1)} %collective-permute-done.2.refs_0_), channel_id=1, source_target_pairs={{0,1},{1,0},{2,3},{3,2},{4,5},{5,4},{6,7},{7,6},{8,9},{9,8},{10,11... | collective-permute-start | bytes 466952 | tf_op jit(solution)/shard_map/ppermute | solution.py:298

commit v6 on v5

--- a/solution.py
+++ b/solution.py
@@ -164,24 +164,22 @@
 
 def add_all(shape, order, blocks, height, offsets_ref, refs, acc, again):
     me = lax.axis_index("ctx").astype(jnp.int32)
-    slots = refs[0].shape[0] // height
-
     def add(ref, s, base, tag, flip):
         source = origin_of(order, me, s, tag, flip)
         add_block(shape, prepare(shape, offsets_ref, ref, base, source), me, acc, again)
 
-    if slots <= 4:
-        for ref, (tag, flip) in zip(refs, blocks):
+    for ref, (tag, flip) in zip(refs, blocks):
+        slots = ref.shape[0] // height
+        if slots <= 4:
             for s in range(slots):
                 add(ref, s, s * height, tag, flip)
-        return
-
-    def step(s, _):
-        for ref, (tag, flip) in zip(refs, blocks):
+            continue
+
+        def step(s, _, ref=ref, tag=tag, flip=flip):
             add(ref, s, pl.multiple_of(s * height, height), tag, flip)
-        return 0
-
-    lax.fori_loop(0, slots, step, 0)
+            return 0
+
+        lax.fori_loop(0, slots, step, 0)
 
 
 def first_kernel(shape, order, blocks, height, offsets_ref, *refs):
@@ -332,18 +330,23 @@
     one = swap(near, last - 1)
     acc = add("sums_got", [(got, 1 << (last - 2), 0)], acc)
     near, late, acc = lax.optimization_barrier((near, got, acc))
-    two = jnp.concatenate([two_early, swap(late, last)], axis=0)
-    near_core = core(near)
+    two_late = swap(late, last)
+    two = jnp.concatenate([two_early, two_late], axis=0)
+    pair = jnp.concatenate([near, two_early], axis=0)
+    pair_core = core(pair)
+    near_core, early_core = pair_core[: near.shape[0]], pair_core[near.shape[0] :]
     one, acc = after(one, acc)
     three = swap(one, last)
     one_core = core(one)
-    blocks = [(one, bits[0], 0), (two, bits[1], 0), (near_core, 0, 1), (one_core, bits[0], 1)]
+    rest = bits[1] | 1 << (last - 2)
+    blocks = [(one, bits[0], 0), (two, bits[1], 0)]
+    blocks += [(near_core, 0, 1), (one_core, bits[0], 1), (early_core, bits[1], 1)]
     acc = add("sums_next", blocks, acc)
-    two, acc = after(two, acc)
-    two_core = core(two)
-    three, acc = after(three, acc)
+    two_late, acc = after(two_late, acc)
+    late_core = core(two_late)
+    three, late_core, acc = lax.optimization_barrier((three, late_core, acc))
     three_core = core(three)
-    acc = add("sums_three", [(three, both, 0), (two_core, bits[1], 1)], acc, fold=True)
+    acc = add("sums_three", [(three, both, 0), (late_core, rest, 1)], acc, fold=True)
     three_core, acc = after(three_core, acc)
     blocks = [(three_core, both, 1)]
     columns = rank * rank // devices

time: 26.6 us -> 26.4 us (level)
  transfers between devices with their start and end apart: 9 -> 9, of which waited for: 3 -> 4; matrix products, arithmetic and copies ran while one was open for 0% -> 0% of each run, Pallas kernels for 17% -> 16%
where the time goes in v6:
time: 26.4 us; the launch traced here: 26.3 us
  starting transfers between devices  11.2 us (42%)
  Pallas kernels  10.7 us (41%)
  waiting for transfers between devices  3.59 us (14%)
  between operations  0.73 us (3%)
    ppermute x5, starting transfers between devices, swap(): lax.ppermute(block, 'ctx', [(i, i ^ order[i & 1][k]) for i in range(devic...  10.8 us
    pallas_call x1, Pallas kernels, on_device(): pl.pallas_call(project_kernel, out_shape=(pltpu.VMEM((height, width), jnp...  4.89 us
    pallas_call x4, Pallas kernels, add(): pl.pallas_call(functools.partial(kernel, shape, order, [b[1:] for b in bl...  4.24 us
    ppermute x5, waiting for transfers between devices, swap(): lax.ppermute(block, 'ctx', [(i, i ^ order[i & 1][k]) for i in range(devic...  3.36 us
    pallas_call x1, Pallas kernels, on_device(): pl.pallas_call(functools.partial(last_kernel, shape, order, [b[1:] for b...  1.62 us
  transfers between devices with their start and end apart: 9, of which 4 were waited for; matrix products, arithmetic and copies ran while one was open for 0% of the time, Pallas kernels for 16%

profile of v6, /device:TPU:0, one launch (start us, length us, event | category | flops | bytes accessed | tf_op | source)
XLA Modules:
  0.0 26.3 jit_solution(11999401333297817375)
XLA Ops:
  0.6 4.9 %project.1 = (bf16[16,2432]{1,0:T(8,128)(2,1)S(1)}, s32[9]{0:T(128)S(4)}) custom-call(f32[8,256]{1,0:T(8,128)} %bitcast.7, s32[8,256]{1,0:T(8,128)} %bitcast.8, s32[9]{0:T(128)} %offsets_hbm.1, bf16[256,7168]{1,0:T(8,128)(2,1)} %x_hbm.1, bf16[256,7168]{1,0:T(8,128)(2,1)} %g_hbm.1, bf16[7168,128]{1,0:T(8,128)(2,1)} %p_hbm.1), custom_call_target="tpu_custom_call" | custom-call | tf_op jit(solution)/shard_map/project/pallas_call | solution.py:264
  5.5 4.1 %collective-permute-start = (bf16[16,2432]{1,0:T(8,128)(2,1)S(1)}, bf16[16,2432]{1,0:T(8,128)(2,1)S(1)}, u32[]{:S(2)}, u32[]{:S(2)}) collective-permute-start(bf16[16,2432]{1,0:T(8,128)(2,1)S(1)} %get-tuple-element.51.refs_0_), channel_id=1, source_target_pairs={{0,8},{1,5},{2,10},{3,7},{4,12},{5,1},{6,14},{7,3},{8,0},{9,13},{1... | collective-permute-start | bytes 233480 | tf_op jit(solution)/shard_map/ppermute | solution.py:293
  9.6 0.6 %sums_own.1 = (f32[8,544,128]{2,1,0:T(8,128)S(1)}, f32[8,544,128]{2,1,0:T(8,128)S(1)}) custom-call(s32[9]{0:T(128)S(4)} %get-tuple-element.34.offsets_ref, bf16[16,2432]{1,0:T(8,128)(2,1)S(1)} %get-tuple-element.51.refs_0_), custom_call_target="tpu_custom_call" | custom-call | tf_op jit(solution)/shard_map/sums_own/pallas_call | solution.py:307
  10.3 1.6 %collective-permute-start.4 = (bf16[16,2432]{1,0:T(8,128)(2,1)S(1)}, bf16[16,2432]{1,0:T(8,128)(2,1)S(1)}, u32[]{:S(2)}, u32[]{:S(2)}) collective-permute-start(bf16[16,2432]{1,0:T(8,128)(2,1)S(1)} %get-tuple-element.51.refs_0_), channel_id=1, source_target_pairs={{0,4},{1,3},{2,6},{3,1},{4,0},{5,7},{6,2},{7,5},{8,12},{9,11},{10,... | collective-permute-start | bytes 233480 | tf_op jit(solution)/shard_map/ppermute | solution.py:293
  11.9 0.1 collective-permute-done.refs_0_
  12.0 1.9 %collective-permute-start.1 = (bf16[32,2432]{1,0:T(8,128)(2,1)S(1)}, bf16[32,2432]{1,0:T(8,128)(2,1)S(1)}, u32[]{:S(2)}, u32[]{:S(2)}) collective-permute-start(bf16[32,2432]{1,0:T(8,128)(2,1)S(1)} %constant_dynamic-update-slice_fusion), channel_id=1, source_target_pairs={{0,2},{1,9},{2,0},{3,11},{4,6},{5,13},{6,4},{7,15},{8,10},{9,1},{1... | collective-permute-start | bytes 466952 | tf_op jit(solution)/shard_map/ppermute | solution.py:293
  13.9 0.4 %sums_got.1 = (f32[8,544,128]{2,1,0:T(8,128)S(1)}, f32[8,544,128]{2,1,0:T(8,128)S(1)}) custom-call(s32[9]{0:T(128)S(4)} %get-tuple-element.34.offsets_ref, f32[8,544,128]{2,1,0:T(8,128)S(1)} %get-tuple-element.41.acc_in, f32[8,544,128]{2,1,0:T(8,128)S(1)} %get-tuple-element.42.again_in, ...), custom_call_target="tpu_custom_call", output_to_operand_aliasing={{0}: (1, {}), {1}: (2, {})} | custom-call | tf_op jit(solution)/shard_map/sums_got/pallas_call | solution.py:307
  14.3 1.6 %collective-permute-start.3 = (bf16[16,2432]{1,0:T(8,128)(2,1)S(1)}, bf16[16,2432]{1,0:T(8,128)(2,1)S(1)}, u32[]{:S(2)}, u32[]{:S(2)}) collective-permute-start(bf16[16,2432]{1,0:T(8,128)(2,1)S(1)} %collective-permute-done.refs_0_), channel_id=1, source_target_pairs={{0,4},{1,3},{2,6},{3,1},{4,0},{5,7},{6,2},{7,5},{8,12},{9,11},{10,... | collective-permute-start | bytes 233480 | tf_op jit(solution)/shard_map/ppermute | solution.py:293
  15.9 0.0 collective-permute-done.4
  15.9 0.1 collective-permute-start.5
  16.0 2.0 %collective-permute-done.1.refs_0_ = bf16[32,2432]{1,0:T(8,128)(2,1)S(1)} collective-permute-done((bf16[32,2432]{1,0:T(8,128)(2,1)S(1)}, bf16[32,2432]{1,0:T(8,128)(2,1)S(1)}, u32[]{:S(2)}, u32[]{:S(2)}) %collective-permute-start.1) | collective-permute-done | bytes 155680 | tf_op jit(solution)/shard_map/ppermute | solution.py:293
  18.0 0.0 collective-permute-start.6
  18.0 1.6 %collective-permute-start.2 = (bf16[32,2432]{1,0:T(8,128)(2,1)S(1)}, bf16[32,2432]{1,0:T(8,128)(2,1)S(1)}, u32[]{:S(2)}, u32[]{:S(2)}) collective-permute-start(bf16[32,2432]{1,0:T(8,128)(2,1)S(1)} %collective-permute-done.1.refs_0_), channel_id=1, source_target_pairs={{0,4},{1,3},{2,6},{3,1},{4,0},{5,7},{6,2},{7,5},{8,12},{9,11},{10,... | collective-permute-start | bytes 466952 | tf_op jit(solution)/shard_map/ppermute | solution.py:293
  19.6 0.0 collective-permute-done.3
  19.6 0.0 collective-permute-done.5
  19.7 0.0 collective-permute-done.6.refs_3_
  19.7 2.1 %sums_next.1 = (f32[8,544,128]{2,1,0:T(8,128)S(1)}, f32[8,544,128]{2,1,0:T(8,128)S(1)}) custom-call(s32[9]{0:T(128)S(4)} %get-tuple-element.34.offsets_ref, f32[8,544,128]{2,1,0:T(8,128)S(1)} %get-tuple-element.49.acc_in, f32[8,544,128]{2,1,0:T(8,128)S(1)} %get-tuple-element.50.again_in, ...), custom_call_target="tpu_custom_call", output_to_operand_aliasing={{0}: (1, {}), {1}: (2, {})} | custom-call | tf_op jit(solution)/shard_map/sums_next/pallas_call | solution.py:307
  21.8 0.2 collective-permute-start.7
  22.0 1.2 %collective-permute-done.2.refs_0_ = bf16[32,2432]{1,0:T(8,128)(2,1)S(1)} collective-permute-done((bf16[32,2432]{1,0:T(8,128)(2,1)S(1)}, bf16[32,2432]{1,0:T(8,128)(2,1)S(1)}, u32[]{:S(2)}, u32[]{:S(2)}) %collective-permute-start.2) | collective-permute-done | bytes 155680 | tf_op jit(solution)/shard_map/ppermute | solution.py:293
  23.3 0.0 collective-permute-done.7.refs_1_
  23.3 0.0 collective-permute-start.8
  23.3 1.1 %sums_three.1.held = f32[8,544,128]{2,1,0:T(8,128)S(1)} custom-call(s32[9]{0:T(128)S(4)} %get-tuple-element.34.offsets_ref, f32[8,544,128]{2,1,0:T(8,128)S(1)} %get-tuple-element.59.acc_in, f32[8,544,128]{2,1,0:T(8,128)S(1)} %get-tuple-element.60.again, bf16[32,2432]{1,0:T(8,128)(2,1)S(1)} %collective-permute-done.2.refs_0_, ...), custom_call_target="tpu_custom_call", output_to_operand_aliasing={{}: (1, {})} | custom-call | tf_op jit(solution)/shard_map/sums_three/pallas_call | solution.py:307
  24.4 0.2 collective-permute-done.8.refs_0_
  24.7 1.6 %sums_last.1 = (f32[512,8,128]{2,1,0:T(8,128)}, f32[8,256]{1,0:T(8,128)}, f32[8,544,128]{2,1,0:T(8,128)S(1)}) custom-call(s32[9]{0:T(128)S(4)} %get-tuple-element.34.offsets_ref, f32[8,544,128]{2,1,0:T(8,128)S(1)} %sums_three.1.held, bf16[32,2432]{1,0:T(8,128)(2,1)S(1)} %collective-permute-done.8.refs_0_), custom_call_target="tpu_custom_call", output_to_operand_aliasing={{2}: (1, {})} | custom-call | tf_op jit(solution)/shard_map/sums_last/pallas_call | solution.py:353
  (6 shorter events, 0.1 us)
Async XLA Ops:
  5.5 6.5 %collective-permute-start = (bf16[16,2432]{1,0:T(8,128)(2,1)S(1)}, bf16[16,2432]{1,0:T(8,128)(2,1)S(1)}, u32[]{:S(2)}, u32[]{:S(2)}) collective-permute-start(bf16[16,2432]{1,0:T(8,128)(2,1)S(1)} %get-tuple-element.51.refs_0_), channel_id=1, source_target_pairs={{0,8},{1,5},{2,10},{3,7},{4,12},{5,1},{6,14},{7,3},{8,0},{9,13},{1... | collective-permute-start | bytes 233480 | tf_op jit(solution)/shard_map/ppermute | solution.py:293
  10.3 5.6 %collective-permute-start.4 = (bf16[16,2432]{1,0:T(8,128)(2,1)S(1)}, bf16[16,2432]{1,0:T(8,128)(2,1)S(1)}, u32[]{:S(2)}, u32[]{:S(2)}) collective-permute-start(bf16[16,2432]{1,0:T(8,128)(2,1)S(1)} %get-tuple-element.51.refs_0_), channel_id=1, source_target_pairs={{0,4},{1,3},{2,6},{3,1},{4,0},{5,7},{6,2},{7,5},{8,12},{9,11},{10,... | collective-permute-start | bytes 233480 | tf_op jit(solution)/shard_map/ppermute | solution.py:293
  12.0 6.0 %collective-permute-start.1 = (bf16[32,2432]{1,0:T(8,128)(2,1)S(1)}, bf16[32,2432]{1,0:T(8,128)(2,1)S(1)}, u32[]{:S(2)}, u32[]{:S(2)}) collective-permute-start(bf16[32,2432]{1,0:T(8,128)(2,1)S(1)} %constant_dynamic-update-slice_fusion), channel_id=1, source_target_pairs={{0,2},{1,9},{2,0},{3,11},{4,6},{5,13},{6,4},{7,15},{8,10},{9,1},{1... | collective-permute-start | bytes 466952 | tf_op jit(solution)/shard_map/ppermute | solution.py:293
  14.3 5.3 %collective-permute-start.3 = (bf16[16,2432]{1,0:T(8,128)(2,1)S(1)}, bf16[16,2432]{1,0:T(8,128)(2,1)S(1)}, u32[]{:S(2)}, u32[]{:S(2)}) collective-permute-start(bf16[16,2432]{1,0:T(8,128)(2,1)S(1)} %collective-permute-done.refs_0_), channel_id=1, source_target_pairs={{0,4},{1,3},{2,6},{3,1},{4,0},{5,7},{6,2},{7,5},{8,12},{9,11},{10,... | collective-permute-start | bytes 233480 | tf_op jit(solution)/shard_map/ppermute | solution.py:293
  15.9 3.7 %collective-permute-start.5 = (bf16[48,2432]{1,0:T(8,128)(2,1)S(1)}, bf16[48,2432]{1,0:T(8,128)(2,1)S(1)}, u32[]{:S(2)}, u32[]{:S(2)}) collective-permute-start(bf16[48,2432]{1,0:T(8,128)(2,1)S(1)} %pad_maximum_fusion), channel_id=1, source_target_pairs={{0,1},{1,0},{2,3},{3,2},{4,5},{5,4},{6,7},{7,6},{8,9},{9,8},{10,11... | collective-permute-start | bytes 700424 | tf_op jit(solution)/shard_map/ppermute | solution.py:296
  18.0 1.6 %collective-permute-start.6 = (bf16[32,2432]{1,0:T(8,128)(2,1)S(1)}, bf16[32,2432]{1,0:T(8,128)(2,1)S(1)}, u32[]{:S(2)}, u32[]{:S(2)}) collective-permute-start(bf16[32,2432]{1,0:T(8,128)(2,1)S(1)} %collective-permute-done.1.refs_0_), channel_id=1, source_target_pairs={{0,1},{1,0},{2,3},{3,2},{4,5},{5,4},{6,7},{7,6},{8,9},{9,8},{10,11... | collective-permute-start | bytes 466952 | tf_op jit(solution)/shard_map/ppermute | solution.py:296
  18.0 5.2 %collective-permute-start.2 = (bf16[32,2432]{1,0:T(8,128)(2,1)S(1)}, bf16[32,2432]{1,0:T(8,128)(2,1)S(1)}, u32[]{:S(2)}, u32[]{:S(2)}) collective-permute-start(bf16[32,2432]{1,0:T(8,128)(2,1)S(1)} %collective-permute-done.1.refs_0_), channel_id=1, source_target_pairs={{0,4},{1,3},{2,6},{3,1},{4,0},{5,7},{6,2},{7,5},{8,12},{9,11},{10,... | collective-permute-start | bytes 466952 | tf_op jit(solution)/shard_map/ppermute | solution.py:293
  21.8 1.5 %collective-permute-start.7 = (bf16[16,2432]{1,0:T(8,128)(2,1)S(1)}, bf16[16,2432]{1,0:T(8,128)(2,1)S(1)}, u32[]{:S(2)}, u32[]{:S(2)}) collective-permute-start(bf16[16,2432]{1,0:T(8,128)(2,1)S(1)} %collective-permute-done.3), channel_id=1, source_target_pairs={{0,1},{1,0},{2,3},{3,2},{4,5},{5,4},{6,7},{7,6},{8,9},{9,8},{10,11... | collective-permute-start | bytes 233480 | tf_op jit(solution)/shard_map/ppermute | solution.py:296
  23.3 1.4 %collective-permute-start.8 = (bf16[32,2432]{1,0:T(8,128)(2,1)S(1)}, bf16[32,2432]{1,0:T(8,128)(2,1)S(1)}, u32[]{:S(2)}, u32[]{:S(2)}) collective-permute-start(bf16[32,2432]{1,0:T(8,128)(2,1)S(1)} %collective-permute-done.2.refs_0_), channel_id=1, source_target_pairs={{0,1},{1,0},{2,3},{3,2},{4,5},{5,4},{6,7},{7,6},{8,9},{9,8},{10,11... | collective-permute-start | bytes 466952 | tf_op jit(solution)/shard_map/ppermute | solution.py:296
